TPU v7x, 512 devices: a whole 4x8x8 slice. The times are simulated.
512 devices in a mesh: met: 8 (over z), mach: 64 (over y, x, core).
Axes of the slice: x: 4, y: 8, z: 8, core: 2. Of those that a mesh axis runs over, the one named last changes fastest.
Arguments:
- tensor: float32 [4, 32768, 2048], P(None, 'mach', 'met'), may hold values from -6 to 6
- metric_factor: float32 [2048, 64], P(('met', 'mach')), may hold values from -0.125 to 0.125
- time_factor: float32 [4, 64], replicated, may hold values from 0.5 to 1.5
Outputs:
- machine_factor: float32 [32768, 64], P(('mach', 'met'))
- residual: float32 [4, 32768, 2048], P(None, 'mach', 'met')
All inputs are finite; a program needn't handle non-finite values.
Results may differ from a plain program's by a relative error of at most 0.000078.
Values sent between devices are 32-bit elements; how exact they have to be, the bound alone decides.
No kernel may reach another device: no remote copies, remote signals or barrier semaphores. Data moves between devices by JAX's collectives and lax.ppermute only.
A program may use at most 64 MiB of HBM per device.

v0:
```python
import jax
import jax.numpy as jnp
from jax import lax
from jax.sharding import PartitionSpec as P


def local(tensor, metric_factor, time_factor):
    highest = lax.Precision.HIGHEST
    metric_block = lax.all_gather(metric_factor, "mach", axis=0, tiled=True)
    khatri_rao = time_factor[:, None, :] * metric_block[None, :, :]
    time_gram = jnp.dot(
        time_factor.T, time_factor, precision=highest, preferred_element_type=jnp.float32
    )
    block_gram = jnp.dot(
        metric_block.T, metric_block, precision=highest, preferred_element_type=jnp.float32
    )
    metric_gram = lax.psum(block_gram, "met")
    cholesky_factor = jnp.linalg.cholesky(metric_gram * time_gram)
    partial_sum = jnp.einsum("kij,kjr->ir", tensor, khatri_rao, precision=highest)
    owned_sums = lax.psum_scatter(partial_sum, "met", scatter_dimension=0, tiled=True)
    own_rows = jax.scipy.linalg.cho_solve((cholesky_factor, True), owned_sums.T).T
    solved = lax.all_gather(own_rows, "met", axis=0, tiled=True)
    rebuilt = jnp.einsum("ir,kjr->kij", solved, khatri_rao, precision=highest)
    return (own_rows, tensor - rebuilt)


def solution(mesh):
    return jax.shard_map(
        local,
        mesh=mesh,
        in_specs=(P(None, "mach", "met"), P(("met", "mach"), None), P()),
        out_specs=(P(("mach", "met"), None), P(None, "mach", "met")),
        check_vma=False,
    )
```

profile of v0, /device:TPU:16, one launch (start us, length us, event | category | flops | bytes accessed | tf_op | source)
XLA Modules:
  0.0 151.2 jit_solution(2834654673776025973)
XLA Ops:
  7.2 0.0 copy-start.2
  7.2 0.0 copy-start
  7.2 0.0 reduce-scatter.4.cloned.1.call-start
  7.2 50.4 %all-gather = f32[64,4,64]{2,1,0:T(4,128)S(1)} all-gather(f32[1,4,64]{2,1,0:T(4,128)} %bitcast.32), channel_id=1, replica_groups=mesh['met'=8,'mach'=64] {'mach'}, dimensions={0}, use_global_device_ids=true | all-gather | bytes 66560 | tf_op jit(solution)/shard_map/all_gather | solution.py:9
  57.6 0.1 copy.14
  57.7 3.7 %convolution_bitcast_fusion = f32[512,64]{0,1:T(8,128)S(1)} fusion(f32[4,512,256]{2,1,0:T(8,128)} %param.3, f32[256,64]{0,1:T(8,128)S(1)} %copy.14, f32[4,64]{1,0:T(4,128)} %param.5), kind=kOutput, calls=%fused_computation.1 | convolution fusion | flops 402718720 | bytes 2294784 | tf_op jit(solution)/shard_map/kij,kjr->ir/dot_general | solution.py:19
  61.4 0.8 copy.19
  62.3 0.0 reduce-scatter.4.cloned.1.call-update
  62.3 0.4 fusion.13
  62.7 35.9 %psum.7 = f32[64,64]{0,1:T(8,128)S(1)} all-reduce(f32[64,64]{0,1:T(8,128)S(1)} %fusion.13), channel_id=1, replica_groups=mesh['met'=8,'mach'=64] {'met'}, use_global_device_ids=true, to_apply=%region_0.0 | all-reduce | flops 4096 | bytes 32768 | tf_op jit(solution)/shard_map/psum | solution.py:17
  98.6 0.0 copy-done.2
  98.6 0.2 convolution_multiply_fusion
  98.8 0.1 copy.13
  98.9 5.8 %cholesky.16 = f32[64,64]{1,0:T(8,128)S(1)} custom-call(f32[64,64]{1,0:T(8,128)S(1)} %fusion.12), custom_call_target="Cholesky" | custom-call | tf_op jit(solution)/shard_map/jit(cholesky)/cholesky | solution.py:18
  104.8 0.6 compare_reduce_fusion
  105.5 0.0 copy-done
  105.5 1.8 %copy.15 = f32[4,512,256]{1,2,0:T(8,128)} copy(f32[4,512,256]{2,1,0:T(8,128)S(1)} %copy-done) | data formatting | bytes 4194304 | tf_op args[0]
  107.3 0.7 fusion.7
  107.9 4.9 %custom-call.10 = f32[1,64,64]{1,2,0:T(8,128)S(1)} custom-call(f32[1,64,64]{2,1,0:T(8,128)S(1)} %fusion.7), custom_call_target="InvertDiagBlocksLowerTriangular" | custom-call | tf_op jit(solution)/shard_map/jit(_cho_solve)/triangular_solve | solution.py:21
  112.8 0.0 reduce-scatter.4.cloned.1.call-done
  112.9 1.0 fusion.10
  113.9 0.2 fusion.8
  114.1 0.0 copy-start.1
  114.1 24.8 %all_gather.7 = f32[512,64]{1,0:T(8,128)S(1)} all-gather(f32[64,64]{1,0:T(8,128)S(1)} %fusion.8), channel_id=1, replica_groups=mesh['met'=8,'mach'=64] {'met'}, dimensions={0}, use_global_device_ids=true | all-gather | bytes 147456 | tf_op jit(solution)/shard_map/all_gather | solution.py:22
  138.9 3.6 %bitcast_subtract_fusion = f32[4,512,256]{1,2,0:T(8,128)S(1)} fusion(f32[4,512,256]{1,2,0:T(8,128)} %copy.15, f32[512,64]{1,0:T(8,128)S(1)} %all_gather.7, f32[256,64]{0,1:T(8,128)S(1)} %copy.14, f32[4,64]{1,0:T(4,128)S(1)} %copy-done.2), kind=kOutput, calls=%fused_computation | convolution fusion | flops 403243008 | bytes 4391936 | tf_op jit(solution)/shard_map/ir,kjr->kij/dot_general | solution.py:23
  142.5 0.0 copy-done.1
  142.5 1.8 %copy.16 = f32[4,512,256]{2,1,0:T(8,128)} copy(f32[4,512,256]{1,2,0:T(8,128)S(1)} %bitcast_subtract_fusion) | data formatting | bytes 4194304
  (2 shorter events, 0.0 us)
Async XLA Ops:
  7.2 91.4 %copy-start.2 = (f32[4,64]{1,0:T(4,128)S(1)}, f32[4,64]{1,0:T(4,128)}, u32[]{:S(2)}) copy-start(f32[4,64]{1,0:T(4,128)} %param.5) | copy-start | bytes 3076
  7.2 98.3 %copy-start = (f32[4,512,256]{2,1,0:T(8,128)S(1)}, f32[4,512,256]{2,1,0:T(8,128)}, u32[]{:S(2)}) copy-start(f32[4,512,256]{2,1,0:T(8,128)} %param.3) | copy-start | bytes 6291460
  7.2 105.7 %reduce-scatter.4.cloned.1.call-start = ((), (), s32[]{:S(2)}) async-start(), calls=%async_computation.1 | async-start | bytes 294912
  114.1 28.4 %copy-start.1 = (f32[64,64]{1,0:T(8,128)}, f32[64,64]{1,0:T(8,128)S(1)}, u32[]{:S(2)}) copy-start(f32[64,64]{1,0:T(8,128)S(1)} %fusion.8) | copy-start | bytes 49156
Sparse Core Ops, SparseCore 0:
  62.4 42.0 reduce-scatter.3
where the time goes:
time: 151 us
  blocking collectives  111 us (74%)
  between operations  14.1 us (9%)
  other arithmetic  12.1 us (8%)
  matrix products  9.14 us (6%)
  local copies, waits for them, and re-layouts  4.62 us (3%)
    all_gather x1, blocking collectives, local(): metric_block = lax.all_gather(metric_factor, 'mach', axis=0, tiled=True)  50.4 us
    psum x1, blocking collectives, local(): metric_gram = lax.psum(block_gram, 'met')  35.9 us
    all_gather x1, blocking collectives, local(): solved = lax.all_gather(own_rows, 'met', axis=0, tiled=True)  24.8 us
    another operation x3, other arithmetic, local(): cholesky_factor = jnp.linalg.cholesky(metric_gram * time_gram)  6.52 us
    another operation x2, other arithmetic, local(): jax.scipy.linalg.cho_solve((cholesky_factor, True), owned_sums.T)  5.55 us
    unnamed x10, local copies, waits for them, and re-layouts  4.54 us
    dot_general x1, matrix products, local(): jnp.einsum('kij,kjr->ir', tensor, khatri_rao, precision=highest)  3.72 us
    dot_general x1, matrix products, local(): rebuilt = jnp.einsum('ir,kjr->kij', solved, khatri_rao, precision=highest)  3.59 us
  transfers between devices with their start and end apart: 1, of which 0 were waited for; matrix products, arithmetic and copies ran while one was open for 10% of the time, Pallas kernels for 0%

commit v1 on v0

v1 whole, which is shorter than its diff:
```python
import jax
import jax.numpy as jnp
from jax import lax
from jax.experimental import pallas as pl
from jax.experimental.pallas import tpu as pltpu
from jax.sharding import PartitionSpec as P

RANK = 64
F32 = jnp.float32
BF16 = jnp.bfloat16
HIGHEST = lax.Precision.HIGHEST
LIMIT = 48 * 1024 * 1024
VMEM = pl.BlockSpec(memory_space=pltpu.VMEM)


def split(x):
    high = x.astype(BF16)
    return high, (x - high.astype(F32)).astype(BF16)


def dot(a, b, contract, precision=None):
    return lax.dot_general(
        a, b, (contract, ((), ())), precision=precision, preferred_element_type=F32
    )


def spread_kernel(m_ref, out_ref):
    rows = m_ref.shape[0]
    packed = jnp.concatenate(
        [
            jnp.concatenate([m_ref[i : i + 1, :], m_ref[i + 1 : i + 2, :]], axis=1)
            for i in range(0, rows, 2)
        ],
        axis=0,
    )
    out_ref[...] = jnp.broadcast_to(packed[None], out_ref.shape)


def sums_kernel(t_ref, g_ref, tf_ref, out_ref, m_ref):
    steps, machines, metrics = t_ref.shape
    parts = out_ref.shape[0]
    own = machines // parts
    half = own // 2
    m_ref[pl.ds(0, metrics // 2, stride=2), :] = g_ref[:, :RANK]
    m_ref[pl.ds(1, metrics // 2, stride=2), :] = g_ref[:, RANK:]
    m = m_ref[...]
    gram = dot(m, m, ((0,), (0,)), HIGHEST)
    gram = jnp.concatenate([gram[: RANK // 2], gram[RANK // 2 :]], axis=1)
    acc = jnp.zeros((machines, 2 * RANK), F32)
    for k in range(steps):
        right = jnp.concatenate(split(m * tf_ref[k : k + 1, :]), axis=1)
        high, low = split(t_ref[k])
        acc = acc + dot(high, right, ((1,), (0,))) + dot(low, right, ((1,), (0,)))
    for c in range(parts):
        block = acc[c * own : (c + 1) * own]
        sums = block[:, :RANK] + block[:, RANK:]
        out_ref[c, :half, :] = jnp.concatenate([sums[:half], sums[half:]], axis=1)
        out_ref[c, half:, :] = gram


def reduce_kernel(r_ref, own_ref, gram_ref):
    parts, rows, _ = r_ref.shape
    total = r_ref[0]
    for c in range(1, parts):
        total = total + r_ref[c]
    own_ref[...] = jnp.broadcast_to(total[None, : rows // 2], own_ref.shape)
    gram_ref[...] = total[rows // 2 :]


def solve_kernel(gram_ref, own_ref, m_ref, tf_ref, w_ref, rows_ref):
    steps = tf_ref.shape[0]
    packed = gram_ref[...]
    gram = jnp.concatenate([packed[:, :RANK], packed[:, RANK:]], axis=0)
    tf = tf_ref[...]
    normal = gram * dot(tf, tf, ((0,), (0,)), HIGHEST)
    row_id = lax.broadcasted_iota(jnp.int32, (RANK, RANK), 0)
    col_id = lax.broadcasted_iota(jnp.int32, (RANK, RANK), 1)
    both = jnp.concatenate([normal, (row_id == col_id).astype(F32)], axis=1)
    blocks = [both[8 * b : 8 * b + 8] for b in range(RANK // 8)]
    sub = lax.broadcasted_iota(jnp.int32, (8, 2 * RANK), 0)
    for j in range(RANK):
        b0, s = divmod(j, 8)
        row = blocks[b0][s : s + 1, :]
        scaled = row / row[:, j : j + 1]
        for b in range(b0, RANK // 8):
            column = jnp.broadcast_to(blocks[b][:, j : j + 1], (8, 2 * RANK))
            if b == b0:
                column = jnp.where(sub > s, column, 0.0)
            blocks[b] = blocks[b] - column * scaled
    done = jnp.concatenate(blocks, axis=0)
    left, right = done[:, :RANK], done[:, RANK:]
    pivots = jnp.sum(jnp.where(row_id == col_id, left, 0.0), axis=1, keepdims=True)
    inverse = right * lax.rsqrt(pivots)
    sums = jnp.concatenate([own_ref[0, :, :RANK], own_ref[0, :, RANK:]], axis=0)
    half = dot(sums, inverse, ((1,), (1,)), HIGHEST)
    rows_ref[...] = dot(half, inverse, ((1,), (0,)), HIGHEST)
    whole = dot(inverse, inverse, ((0,), (0,)), HIGHEST)
    m = m_ref[...]
    for k in range(steps):
        high, low = split(dot(whole, m * tf_ref[k : k + 1, :], ((1,), (1,)), HIGHEST))
        w_ref[k] = jnp.concatenate([high, high, low, low], axis=0)


def residual_kernel(t_ref, s_ref, w_ref, out_ref):
    packed = s_ref[...].reshape(s_ref.shape[0] * s_ref.shape[1], 2 * RANK)
    half = s_ref.shape[1]
    pieces = []
    for c in range(s_ref.shape[0]):
        block = packed[c * half : (c + 1) * half]
        pieces += [block[:, :RANK], block[:, RANK:]]
    high, low = split(jnp.concatenate(pieces, axis=0))
    left = jnp.concatenate([high, low, high, low], axis=1)
    for k in range(t_ref.shape[0]):
        out_ref[k] = t_ref[k] - dot(left, w_ref[k], ((1,), (0,)))


def local(parts, plane, tensor, metric_factor, time_factor):
    steps, machines, metrics = tensor.shape
    own = machines // parts
    params = pltpu.CompilerParams(vmem_limit_bytes=LIMIT)
    rows = metric_factor.shape[0]
    copies = pl.pallas_call(
        spread_kernel,
        out_shape=jax.ShapeDtypeStruct((plane, rows // 2, 2 * RANK), F32),
        in_specs=[VMEM],
        out_specs=VMEM,
    )(metric_factor)
    gathered = lax.all_to_all(copies, "mach", 0, 0).reshape(metrics // 2, 2 * RANK)
    partial, metric_block = pl.pallas_call(
        sums_kernel,
        out_shape=(
            jax.ShapeDtypeStruct((parts, own, 2 * RANK), F32),
            jax.ShapeDtypeStruct((metrics, RANK), F32),
        ),
        in_specs=[VMEM] * 3,
        out_specs=(VMEM, VMEM),
        compiler_params=params,
    )(tensor, gathered, time_factor)
    received = lax.all_to_all(partial, "met", 0, 0)
    own_sums, gram = pl.pallas_call(
        reduce_kernel,
        out_shape=(
            jax.ShapeDtypeStruct((parts, own // 2, 2 * RANK), F32),
            jax.ShapeDtypeStruct((RANK // 2, 2 * RANK), F32),
        ),
        in_specs=[VMEM],
        out_specs=(VMEM, VMEM),
    )(received)
    sums = lax.all_to_all(own_sums, "met", 0, 0)
    weights, own_rows = pl.pallas_call(
        solve_kernel,
        out_shape=(
            jax.ShapeDtypeStruct((steps, 4 * RANK, metrics), BF16),
            jax.ShapeDtypeStruct((own, RANK), F32),
        ),
        in_specs=[VMEM] * 4,
        out_specs=(VMEM, VMEM),
        compiler_params=params,
        cost_estimate=pl.CostEstimate(flops=10**9, bytes_accessed=10**7, transcendentals=0),
    )(gram, own_sums, metric_block, time_factor)
    residual = pl.pallas_call(
        residual_kernel,
        out_shape=jax.ShapeDtypeStruct(tensor.shape, F32),
        in_specs=[VMEM] * 3,
        out_specs=VMEM,
        compiler_params=params,
    )(tensor, sums, weights)
    return own_rows, residual


def solution(mesh):
    def run(tensor, metric_factor, time_factor):
        return local(mesh.shape["met"], mesh.shape["mach"], tensor, metric_factor, time_factor)

    return jax.shard_map(
        run,
        mesh=mesh,
        in_specs=(P(None, "mach", "met"), P(("met", "mach"), None), P()),
        out_specs=(P(("mach", "met"), None), P(None, "mach", "met")),
        check_vma=False,
    )
```

time: 151 us -> 64.1 us (0.42)
  the two profiles are of different devices: /device:TPU:16 before, /device:TPU:1 now
where the time goes in v1:
time: 64.1 us; the launch traced here: 63.6 us
  blocking collectives  42.6 us (66%)
  Pallas kernels  13 us (20%)
  local copies, waits for them, and re-layouts  3.93 us (6%)
  starting transfers between devices  3.37 us (5%)
  between operations  0.69 us (1%)
    all_to_all x1, blocking collectives, local(): lax.all_to_all(copies, 'mach', 0, 0).reshape(metrics // 2, 2 * RANK)  21.7 us
    all_to_all x1, blocking collectives, local(): received = lax.all_to_all(partial, 'met', 0, 0)  20.9 us
    pallas_call x1, Pallas kernels, local(): pl.pallas_call(solve_kernel, out_shape=(jax.ShapeDtypeStruct((steps, 4 *...  6.79 us
    unnamed x12, local copies, waits for them, and re-layouts  3.93 us
    all_to_all x1, starting transfers between devices, local(): sums = lax.all_to_all(own_sums, 'met', 0, 0)  3.37 us
    pallas_call x1, Pallas kernels, local(): pl.pallas_call(residual_kernel, out_shape=jax.ShapeDtypeStruct(tensor.sha...  1.95 us
    pallas_call x1, Pallas kernels, local(): pl.pallas_call(reduce_kernel, out_shape=(jax.ShapeDtypeStruct((parts, own...  1.77 us
    pallas_call x1, Pallas kernels, local(): pl.pallas_call(spread_kernel, out_shape=jax.ShapeDtypeStruct((plane, rows...  1.4 us
  transfers between devices with their start and end apart: 1, of which 0 were waited for; matrix products, arithmetic and copies ran while one was open for 0% of the time, Pallas kernels for 11%

profile of v1, /device:TPU:1, one launch (start us, length us, event | category | flops | bytes accessed | tf_op | source)
XLA Modules:
  0.0 63.6 jit_solution(4043070691106405875)
XLA Ops:
  0.6 0.0 copy-start.4
  0.6 1.4 %shard_map.50 = f32[64,2,128]{2,1,0:T(2,128)} custom-call(f32[4,64]{1,0:T(4,128)} %m_ref.1), custom_call_target="tpu_custom_call" | custom-call | tf_op jit(solution)/shard_map/pallas_call | solution.py:122
  2.0 21.7 %all_to_all.15 = f32[64,2,128]{2,1,0:T(2,128)S(1)} all-to-all(f32[64,2,128]{2,1,0:T(2,128)} %shard_map.50), channel_id=1, replica_groups=mesh['met'=8,'mach'=64] {'mach'}, dimensions={0} | all-to-all | bytes 131072 | tf_op jit(solution)/shard_map/all_to_all | solution.py:128
  23.8 0.0 copy-start
  23.8 1.6 %copy-done = f32[4,512,256]{2,1,0:T(8,128)S(1)} copy-done((f32[4,512,256]{2,1,0:T(8,128)S(1)}, f32[4,512,256]{2,1,0:T(8,128)}, u32[]{:S(2)}) %copy-start) | copy-done | bytes 2097176
  25.3 0.0 copy-start.3
  25.3 0.7 %copy-done.3 = f32[4,64]{1,0:T(4,128)S(1)} copy-done((f32[4,64]{1,0:T(4,128)S(1)}, f32[4,64]{1,0:T(4,128)}, u32[]{:S(2)}) %copy-start.3) | copy-done | bytes 1048
  26.0 1.1 %shard_map.51 = (f32[8,64,128]{2,1,0:T(8,128)S(1)}, f32[256,64]{1,0:T(8,128)S(1)}) custom-call(f32[4,512,256]{2,1,0:T(8,128)S(1)} %copy-done, f32[128,128]{1,0:T(8,128)S(1)} %bitcast.1, f32[4,64]{1,0:T(4,128)S(1)} %copy-done.3), custom_call_target="tpu_custom_call" | custom-call | tf_op jit(solution)/shard_map/pallas_call | solution.py:129
  27.1 20.9 %all_to_all.16.r_ref = f32[8,64,128]{2,1,0:T(8,128)} all-to-all(f32[8,64,128]{2,1,0:T(8,128)S(1)} %get-tuple-element.8), channel_id=1, replica_groups=mesh['met'=8,'mach'=64] {'met'}, dimensions={0} | all-to-all | bytes 524288 | tf_op jit(solution)/shard_map/all_to_all | solution.py:139
  48.0 0.0 copy-start.1
  48.0 1.8 %shard_map.52 = (f32[8,32,128]{2,1,0:T(8,128)}, f32[32,128]{1,0:T(8,128)}) custom-call(f32[8,64,128]{2,1,0:T(8,128)} %all_to_all.16.r_ref), custom_call_target="tpu_custom_call" | custom-call | tf_op jit(solution)/shard_map/pallas_call | solution.py:140
  49.8 3.4 %all-to-all-start.2 = ((f32[8,32,128]{2,1,0:T(8,128)}), f32[8,32,128]{2,1,0:T(8,128)S(1)}, u32[]{:S(2)}, u32[]{:S(2)}) async-start(f32[8,32,128]{2,1,0:T(8,128)} %get-tuple-element.10.own_ref), calls=%async_computation.2 | async-start | bytes 262144 | tf_op jit(solution)/shard_map/all_to_all | solution.py:149
  53.2 0.0 copy-done.4
  53.2 0.0 copy-start.2
  53.2 0.9 %copy-done.2 = f32[8,32,128]{2,1,0:T(8,128)S(1)} copy-done((f32[8,32,128]{2,1,0:T(8,128)S(1)}, f32[8,32,128]{2,1,0:T(8,128)}, u32[]{:S(2)}) %copy-start.2) | copy-done | bytes 131096
  54.1 0.0 copy-start.5
  54.1 0.7 %copy-done.5 = f32[32,128]{1,0:T(8,128)S(1)} copy-done((f32[32,128]{1,0:T(8,128)S(1)}, f32[32,128]{1,0:T(8,128)}, u32[]{:S(2)}) %copy-start.5) | copy-done | bytes 16408
  54.8 6.8 %shard_map.53 = (bf16[4,256,256]{2,1,0:T(8,128)(2,1)S(1)}, f32[64,64]{1,0:T(8,128)}) custom-call(f32[32,128]{1,0:T(8,128)S(1)} %copy-done.5, f32[8,32,128]{2,1,0:T(8,128)S(1)} %copy-done.2, f32[256,64]{1,0:T(8,128)S(1)} %get-tuple-element.11.m_ref, f32[4,64]{1,0:T(4,128)S(1)} %copy-done.4), custom_call_target="tpu_custom_call" | custom-call | flops 1000000000 | bytes 10000000 | tf_op jit(solution)/shard_map/pallas_call | solution.py:150
  61.7 0.0 all-to-all-done.2.s_ref
  61.7 0.0 copy-done.1
  61.7 1.9 %shard_map.54 = f32[4,512,256]{2,1,0:T(8,128)} custom-call(f32[4,512,256]{2,1,0:T(8,128)S(1)} %copy-done.1, f32[8,32,128]{2,1,0:T(8,128)S(1)} %all-to-all-done.2.s_ref, bf16[4,256,256]{2,1,0:T(8,128)(2,1)S(1)} %get-tuple-element.13.w_ref), custom_call_target="tpu_custom_call" | custom-call | tf_op jit(solution)/shard_map/pallas_call | solution.py:161
Async XLA Ops:
  0.6 52.6 %copy-start.4 = (f32[4,64]{1,0:T(4,128)S(1)}, f32[4,64]{1,0:T(4,128)}, u32[]{:S(2)}) copy-start(f32[4,64]{1,0:T(4,128)} %tf_ref.3) | copy-start | bytes 3076
  23.8 1.6 %copy-start = (f32[4,512,256]{2,1,0:T(8,128)S(1)}, f32[4,512,256]{2,1,0:T(8,128)}, u32[]{:S(2)}) copy-start(f32[4,512,256]{2,1,0:T(8,128)} %t_ref.3) | copy-start | bytes 6291460
  25.3 0.7 %copy-start.3 = (f32[4,64]{1,0:T(4,128)S(1)}, f32[4,64]{1,0:T(4,128)}, u32[]{:S(2)}) copy-start(f32[4,64]{1,0:T(4,128)} %tf_ref.3) | copy-start | bytes 3076
  48.0 13.6 %copy-start.1 = (f32[4,512,256]{2,1,0:T(8,128)S(1)}, f32[4,512,256]{2,1,0:T(8,128)}, u32[]{:S(2)}) copy-start(f32[4,512,256]{2,1,0:T(8,128)} %t_ref.3) | copy-start | bytes 6291460
  49.8 11.9 %all-to-all-start.2 = ((f32[8,32,128]{2,1,0:T(8,128)}), f32[8,32,128]{2,1,0:T(8,128)S(1)}, u32[]{:S(2)}, u32[]{:S(2)}) async-start(f32[8,32,128]{2,1,0:T(8,128)} %get-tuple-element.10.own_ref), calls=%async_computation.2 | async-start | bytes 262144 | tf_op jit(solution)/shard_map/all_to_all | solution.py:149
  53.2 0.9 %copy-start.2 = (f32[8,32,128]{2,1,0:T(8,128)S(1)}, f32[8,32,128]{2,1,0:T(8,128)}, u32[]{:S(2)}) copy-start(f32[8,32,128]{2,1,0:T(8,128)} %get-tuple-element.10.own_ref) | copy-start | bytes 393220
  54.1 0.7 %copy-start.5 = (f32[32,128]{1,0:T(8,128)S(1)}, f32[32,128]{1,0:T(8,128)}, u32[]{:S(2)}) copy-start(f32[32,128]{1,0:T(8,128)} %get-tuple-element.9.gram_ref) | copy-start | bytes 49156

commit v2 on v1

--- a/solution.py
+++ b/solution.py
@@ -9,8 +9,19 @@
 F32 = jnp.float32
 BF16 = jnp.bfloat16
 HIGHEST = lax.Precision.HIGHEST
-LIMIT = 48 * 1024 * 1024
 VMEM = pl.BlockSpec(memory_space=pltpu.VMEM)
+PIECE = 128
+PLANE_FIRST = 37
+SUMS_FIRST = 7
+ROWS_FIRST = 7
+
+
+def params(mebibytes):
+    return pltpu.CompilerParams(vmem_limit_bytes=mebibytes * 1024 * 1024)
+
+
+def work(flops):
+    return pl.CostEstimate(flops=flops, bytes_accessed=10**7, transcendentals=0)
 
 
 def split(x):
@@ -36,26 +47,39 @@
     out_ref[...] = jnp.broadcast_to(packed[None], out_ref.shape)
 
 
-def sums_kernel(t_ref, g_ref, tf_ref, out_ref, m_ref):
-    steps, machines, metrics = t_ref.shape
+def prepare_kernel(t_ref, tf_ref, high_ref, low_ref, times_ref, gram_ref):
+    for k in range(t_ref.shape[0]):
+        high_ref[k], low_ref[k] = split(t_ref[k])
+    tf = tf_ref[...]
+    times_ref[...] = tf
+    gram_ref[...] = dot(tf, tf, ((0,), (0,)), HIGHEST)
+
+
+def sums_kernel(high_ref, low_ref, g_ref, tf_ref, out_ref, m_ref):
+    steps, machines, metrics = high_ref.shape
     parts = out_ref.shape[0]
     own = machines // parts
     half = own // 2
-    m_ref[pl.ds(0, metrics // 2, stride=2), :] = g_ref[:, :RANK]
-    m_ref[pl.ds(1, metrics // 2, stride=2), :] = g_ref[:, RANK:]
+    cut = 2 * PLANE_FIRST
+    top = metrics // 2 - cut
+    for h in range(2):
+        lanes = slice(h * RANK, (h + 1) * RANK)
+        m_ref[pl.ds(2 * cut + h, top, stride=2), :] = g_ref[:top, lanes]
+        m_ref[pl.ds(h, cut, stride=2), :] = g_ref[top:, lanes]
     m = m_ref[...]
     gram = dot(m, m, ((0,), (0,)), HIGHEST)
     gram = jnp.concatenate([gram[: RANK // 2], gram[RANK // 2 :]], axis=1)
     acc = jnp.zeros((machines, 2 * RANK), F32)
     for k in range(steps):
         right = jnp.concatenate(split(m * tf_ref[k : k + 1, :]), axis=1)
-        high, low = split(t_ref[k])
-        acc = acc + dot(high, right, ((1,), (0,))) + dot(low, right, ((1,), (0,)))
-    for c in range(parts):
+        acc = acc + dot(high_ref[k], right, ((1,), (0,)))
+        acc = acc + dot(low_ref[k], right, ((1,), (0,)))
+    for i in range(parts):
+        c = (i + SUMS_FIRST) % parts
         block = acc[c * own : (c + 1) * own]
         sums = block[:, :RANK] + block[:, RANK:]
-        out_ref[c, :half, :] = jnp.concatenate([sums[:half], sums[half:]], axis=1)
-        out_ref[c, half:, :] = gram
+        out_ref[i, :half, :] = jnp.concatenate([sums[:half], sums[half:]], axis=1)
+        out_ref[i, half:, :] = gram
 
 
 def reduce_kernel(r_ref, own_ref, gram_ref):
@@ -67,12 +91,11 @@
     gram_ref[...] = total[rows // 2 :]
 
 
-def solve_kernel(gram_ref, own_ref, m_ref, tf_ref, w_ref, rows_ref):
+def solve_kernel(gram_ref, own_ref, m_ref, tf_ref, times_ref, w_ref, rows_ref):
     steps = tf_ref.shape[0]
     packed = gram_ref[...]
     gram = jnp.concatenate([packed[:, :RANK], packed[:, RANK:]], axis=0)
-    tf = tf_ref[...]
-    normal = gram * dot(tf, tf, ((0,), (0,)), HIGHEST)
+    normal = gram * times_ref[...]
     row_id = lax.broadcasted_iota(jnp.int32, (RANK, RANK), 0)
     col_id = lax.broadcasted_iota(jnp.int32, (RANK, RANK), 1)
     both = jnp.concatenate([normal, (row_id == col_id).astype(F32)], axis=1)
@@ -101,42 +124,69 @@
         w_ref[k] = jnp.concatenate([high, high, low, low], axis=0)
 
 
-def residual_kernel(t_ref, s_ref, w_ref, out_ref):
-    packed = s_ref[...].reshape(s_ref.shape[0] * s_ref.shape[1], 2 * RANK)
-    half = s_ref.shape[1]
-    pieces = []
-    for c in range(s_ref.shape[0]):
-        block = packed[c * half : (c + 1) * half]
-        pieces += [block[:, :RANK], block[:, RANK:]]
-    high, low = split(jnp.concatenate(pieces, axis=0))
-    left = jnp.concatenate([high, low, high, low], axis=1)
-    for k in range(t_ref.shape[0]):
-        out_ref[k] = t_ref[k] - dot(left, w_ref[k], ((1,), (0,)))
+def residual_kernel(t_ref, s_ref, w_ref, out_ref, held, sems):
+    parts, half, _ = s_ref.shape
+    steps, machines, _ = t_ref.shape
+    copies = []
+    per = PIECE // (2 * half)
+    for p in range(machines // PIECE):
+        pieces = []
+        for c in range(p * per, (p + 1) * per):
+            block = s_ref[(c - ROWS_FIRST) % parts]
+            pieces += [block[:, :RANK], block[:, RANK:]]
+        high, low = split(jnp.concatenate(pieces, axis=0))
+        left = jnp.concatenate([high, low, high, low], axis=1)
+        rows = pl.ds(p * PIECE, PIECE)
+        for k in range(steps):
+            held[k, rows, :] = t_ref[k, rows, :] - dot(left, w_ref[k], ((1,), (0,)))
+            copy = pltpu.make_async_copy(
+                held.at[k, rows, :], out_ref.at[k, rows, :], sems.at[p, k]
+            )
+            copy.start()
+            copies.append(copy)
+    for copy in copies:
+        copy.wait()
 
 
 def local(parts, plane, tensor, metric_factor, time_factor):
     steps, machines, metrics = tensor.shape
     own = machines // parts
-    params = pltpu.CompilerParams(vmem_limit_bytes=LIMIT)
     rows = metric_factor.shape[0]
+    plane_order = [[(i + PLANE_FIRST) % plane for i in range(plane)]]
+    sums_order = [[(i + SUMS_FIRST) % parts for i in range(parts)]]
+    rows_order = [[(i + ROWS_FIRST) % parts for i in range(parts)]]
     copies = pl.pallas_call(
         spread_kernel,
         out_shape=jax.ShapeDtypeStruct((plane, rows // 2, 2 * RANK), F32),
         in_specs=[VMEM],
         out_specs=VMEM,
+        compiler_params=params(2),
     )(metric_factor)
-    gathered = lax.all_to_all(copies, "mach", 0, 0).reshape(metrics // 2, 2 * RANK)
+    gathered = lax.all_to_all(copies, "mach", 0, 0, axis_index_groups=plane_order).reshape(metrics // 2, 2 * RANK)
+    high, low, times, time_gram = pl.pallas_call(
+        prepare_kernel,
+        out_shape=(
+            jax.ShapeDtypeStruct(tensor.shape, BF16),
+            jax.ShapeDtypeStruct(tensor.shape, BF16),
+            jax.ShapeDtypeStruct(time_factor.shape, F32),
+            jax.ShapeDtypeStruct((RANK, RANK), F32),
+        ),
+        in_specs=[VMEM] * 2,
+        out_specs=(VMEM,) * 4,
+        compiler_params=params(12),
+        cost_estimate=work(10**9),
+    )(tensor, time_factor)
     partial, metric_block = pl.pallas_call(
         sums_kernel,
         out_shape=(
             jax.ShapeDtypeStruct((parts, own, 2 * RANK), F32),
             jax.ShapeDtypeStruct((metrics, RANK), F32),
         ),
-        in_specs=[VMEM] * 3,
+        in_specs=[VMEM] * 4,
         out_specs=(VMEM, VMEM),
-        compiler_params=params,
-    )(tensor, gathered, time_factor)
-    received = lax.all_to_all(partial, "met", 0, 0)
+        compiler_params=params(12),
+    )(high, low, gathered, times)
+    received = lax.all_to_all(partial, "met", 0, 0, axis_index_groups=sums_order)
     own_sums, gram = pl.pallas_call(
         reduce_kernel,
         out_shape=(
@@ -145,25 +195,30 @@
         ),
         in_specs=[VMEM],
         out_specs=(VMEM, VMEM),
+        compiler_params=params(4),
     )(received)
-    sums = lax.all_to_all(own_sums, "met", 0, 0)
+    sums = lax.all_to_all(own_sums, "met", 0, 0, axis_index_groups=rows_order)
     weights, own_rows = pl.pallas_call(
         solve_kernel,
         out_shape=(
             jax.ShapeDtypeStruct((steps, 4 * RANK, metrics), BF16),
             jax.ShapeDtypeStruct((own, RANK), F32),
         ),
-        in_specs=[VMEM] * 4,
+        in_specs=[VMEM] * 5,
         out_specs=(VMEM, VMEM),
-        compiler_params=params,
-        cost_estimate=pl.CostEstimate(flops=10**9, bytes_accessed=10**7, transcendentals=0),
-    )(gram, own_sums, metric_block, time_factor)
+        compiler_params=params(8),
+        cost_estimate=work(10**9),
+    )(gram, own_sums, metric_block, times, time_gram)
     residual = pl.pallas_call(
         residual_kernel,
         out_shape=jax.ShapeDtypeStruct(tensor.shape, F32),
         in_specs=[VMEM] * 3,
-        out_specs=VMEM,
-        compiler_params=params,
+        out_specs=pl.BlockSpec(memory_space=pl.ANY),
+        scratch_shapes=[
+            pltpu.VMEM(tensor.shape, F32),
+            pltpu.SemaphoreType.DMA((machines // PIECE, steps)),
+        ],
+        compiler_params=params(12),
     )(tensor, sums, weights)
     return own_rows, residual
 

time: 64.1 us -> 54.8 us (0.85)
  blocking collectives: 42.6 us -> 14.4 us
  starting transfers between devices: 3.37 us -> 23.7 us
  local copies, waits for them, and re-layouts: 3.93 us -> 2.95 us
    all_to_all x2 -> x1, blocking collectives: 42.6 us -> 14.4 us  [local(): lax.all_to_all(partial, 'met', 0, 0, axis_index_groups=sums_order)]
    all_to_all x1 -> x2, starting transfers between devices: 3.37 us -> 23.7 us  [the longest x1 16.5 us: local(): lax.all_to_all(copies, 'mach', 0, 0, axis_index_groups=plane_order)]
    pallas_call x1, Pallas kernels: 1.77 us -> 0.67 us  [local(): pl.pallas_call(reduce_kernel, out_shape=(jax.ShapeDtypeStruct((parts, own...]
    unnamed x12 -> x8, local copies, waits for them, and re-layouts: 3.93 us -> 2.95 us
    pallas_call x1, Pallas kernels: 6.79 us -> 7.51 us  [local(): pl.pallas_call(solve_kernel, out_shape=(jax.ShapeDtypeStruct((steps, 4 *...]
    pallas_call x0 -> x1, Pallas kernels: none -> 0.7 us  [local(): pl.pallas_call(prepare_kernel, out_shape=(jax.ShapeDtypeStruct(tensor.sha...]
    pallas_call x1, Pallas kernels: 1.4 us -> 0.72 us  [local(): pl.pallas_call(spread_kernel, out_shape=jax.ShapeDtypeStruct((plane, rows...]
  transfers between devices with their start and end apart: 1 -> 2, of which waited for: 0 -> 0; matrix products, arithmetic and copies ran while one was open for 0% -> 0% of each run, Pallas kernels for 11% -> 15%
where the time goes in v2:
time: 54.8 us; the launch traced here: 54.2 us
  starting transfers between devices  23.7 us (43%)
  blocking collectives  14.4 us (26%)
  Pallas kernels  12.4 us (23%)
  local copies, waits for them, and re-layouts  2.95 us (5%)
  between operations  0.7 us (1%)
    all_to_all x1, starting transfers between devices, local(): lax.all_to_all(copies, 'mach', 0, 0, axis_index_groups=plane_order)  16.5 us
    all_to_all x1, blocking collectives, local(): lax.all_to_all(partial, 'met', 0, 0, axis_index_groups=sums_order)  14.4 us
    pallas_call x1, Pallas kernels, local(): pl.pallas_call(solve_kernel, out_shape=(jax.ShapeDtypeStruct((steps, 4 *...  7.51 us
    all_to_all x1, starting transfers between devices, local(): sums = lax.all_to_all(own_sums, 'met', 0, 0, axis_index_groups=rows_order)  7.21 us
    unnamed x8, local copies, waits for them, and re-layouts  2.95 us
    pallas_call x1, Pallas kernels, local(): pl.pallas_call(residual_kernel, out_shape=jax.ShapeDtypeStruct(tensor.sha...  1.76 us
  transfers between devices with their start and end apart: 2, of which 0 were waited for; matrix products, arithmetic and copies ran while one was open for 0% of the time, Pallas kernels for 15%

profile of v2, /device:TPU:1, one launch (start us, length us, event | category | flops | bytes accessed | tf_op | source)
XLA Modules:
  0.0 54.2 jit_solution(5794432509512062446)
XLA Ops:
  0.6 0.0 copy-start.2
  0.6 0.7 %copy-done.2 = f32[4,64]{1,0:T(4,128)S(1)} copy-done((f32[4,64]{1,0:T(4,128)S(1)}, f32[4,64]{1,0:T(4,128)}, u32[]{:S(2)}) %copy-start.2) | copy-done | bytes 1048
  1.3 0.7 %shard_map.51 = f32[64,2,128]{2,1,0:T(2,128)} custom-call(f32[4,64]{1,0:T(4,128)S(1)} %copy-done.2), custom_call_target="tpu_custom_call" | custom-call | tf_op jit(solution)/shard_map/pallas_call | solution.py:158
  2.0 16.5 %all-to-all-start = ((f32[64,2,128]{2,1,0:T(2,128)}), f32[64,2,128]{2,1,0:T(2,128)S(1)}, u32[]{:S(2)}, u32[]{:S(2)}) async-start(f32[64,2,128]{2,1,0:T(2,128)} %shard_map.51), calls=%async_computation | async-start | bytes 131072 | tf_op jit(solution)/shard_map/all_to_all | solution.py:165
  18.5 0.0 copy-start
  18.5 1.6 %copy-done = f32[4,512,256]{2,1,0:T(8,128)S(1)} copy-done((f32[4,512,256]{2,1,0:T(8,128)S(1)}, f32[4,512,256]{2,1,0:T(8,128)}, u32[]{:S(2)}) %copy-start) | copy-done | bytes 2097176
  20.1 0.0 copy-start.3
  20.1 0.7 %copy-done.3 = f32[4,64]{1,0:T(4,128)S(1)} copy-done((f32[4,64]{1,0:T(4,128)S(1)}, f32[4,64]{1,0:T(4,128)}, u32[]{:S(2)}) %copy-start.3) | copy-done | bytes 1048
  20.8 0.7 %shard_map.50 = (bf16[4,512,256]{2,1,0:T(8,128)(2,1)S(1)}, bf16[4,512,256]{2,1,0:T(8,128)(2,1)S(1)}, f32[4,64]{1,0:T(4,128)S(1)}, f32[64,64]{1,0:T(8,128)S(1)}) custom-call(f32[4,512,256]{2,1,0:T(8,128)S(1)} %copy-done, f32[4,64]{1,0:T(4,128)S(1)} %copy-done.3), custom_call_target="tpu_custom_call" | custom-call | flops 1000000000 | bytes 10000000 | tf_op jit(solution)/shard_map/pallas_call | solution.py:166
  21.5 0.0 all-to-all-done
  21.5 1.1 %shard_map.52 = (f32[8,64,128]{2,1,0:T(8,128)S(1)}, f32[256,64]{1,0:T(8,128)S(1)}) custom-call(bf16[4,512,256]{2,1,0:T(8,128)(2,1)S(1)} %get-tuple-element.12.high_ref, bf16[4,512,256]{2,1,0:T(8,128)(2,1)S(1)} %get-tuple-element.13.low_ref, f32[128,128]{1,0:T(8,128)S(1)} %bitcast.1, f32[4,64]{1,0:T(4,128)S(1)} %get-tuple-element.14.tf_ref), custom_call_target="tpu_custom_call" | custom-call | tf_op jit(solution)/shard_map/pallas_call | solution.py:179
  22.6 14.4 %all_to_all.15.r_ref = f32[8,64,128]{2,1,0:T(8,128)S(1)} all-to-all(f32[8,64,128]{2,1,0:T(8,128)S(1)} %get-tuple-element.15), channel_id=1, replica_groups={{448,0,64,128,192,256,320,384},{449,1,65,129,193,257,321,385},{450,2,66..., dimensions={0} | all-to-all | bytes 524288 | tf_op jit(solution)/shard_map/all_to_all | solution.py:189
  37.0 0.0 copy-start.1
  37.0 0.7 %shard_map.53 = (f32[8,32,128]{2,1,0:T(8,128)}, f32[32,128]{1,0:T(8,128)S(1)}) custom-call(f32[8,64,128]{2,1,0:T(8,128)S(1)} %all_to_all.15.r_ref), custom_call_target="tpu_custom_call" | custom-call | tf_op jit(solution)/shard_map/pallas_call | solution.py:190
  37.7 7.2 %all-to-all-start.2 = ((f32[8,32,128]{2,1,0:T(8,128)}), f32[8,32,128]{2,1,0:T(8,128)S(1)}, u32[]{:S(2)}, u32[]{:S(2)}) async-start(f32[8,32,128]{2,1,0:T(8,128)} %get-tuple-element.17.own_ref), calls=%async_computation.2 | async-start | bytes 262144 | tf_op jit(solution)/shard_map/all_to_all | solution.py:200
  44.9 7.5 %shard_map.54 = (bf16[4,256,256]{2,1,0:T(8,128)(2,1)S(1)}, f32[64,64]{1,0:T(8,128)}) custom-call(f32[32,128]{1,0:T(8,128)S(1)} %get-tuple-element.16.gram_ref, f32[8,32,128]{2,1,0:T(8,128)} %get-tuple-element.17.own_ref, f32[256,64]{1,0:T(8,128)S(1)} %get-tuple-element.18.m_ref, f32[4,64]{1,0:T(4,128)S(1)} %get-tuple-element.14.tf_ref, ...), custom_call_target="tpu_custom_call" | custom-call | flops 1000000000 | bytes 10000000 | tf_op jit(solution)/shard_map/pallas_call | solution.py:201
  52.4 0.0 all-to-all-done.2.s_ref
  52.4 0.0 copy-done.1
  52.4 1.8 %shard_map.55 = f32[4,512,256]{2,1,0:T(8,128)} custom-call(f32[4,512,256]{2,1,0:T(8,128)S(1)} %copy-done.1, f32[8,32,128]{2,1,0:T(8,128)S(1)} %all-to-all-done.2.s_ref, bf16[4,256,256]{2,1,0:T(8,128)(2,1)S(1)} %get-tuple-element.21.w_ref), custom_call_target="tpu_custom_call" | custom-call | tf_op jit(solution)/shard_map/pallas_call | solution.py:212
Async XLA Ops:
  0.6 0.7 %copy-start.2 = (f32[4,64]{1,0:T(4,128)S(1)}, f32[4,64]{1,0:T(4,128)}, u32[]{:S(2)}) copy-start(f32[4,64]{1,0:T(4,128)} %m_ref.1) | copy-start | bytes 3076
  2.0 19.5 %all-to-all-start = ((f32[64,2,128]{2,1,0:T(2,128)}), f32[64,2,128]{2,1,0:T(2,128)S(1)}, u32[]{:S(2)}, u32[]{:S(2)}) async-start(f32[64,2,128]{2,1,0:T(2,128)} %shard_map.51), calls=%async_computation | async-start | bytes 131072 | tf_op jit(solution)/shard_map/all_to_all | solution.py:165
  18.5 1.6 %copy-start = (f32[4,512,256]{2,1,0:T(8,128)S(1)}, f32[4,512,256]{2,1,0:T(8,128)}, u32[]{:S(2)}) copy-start(f32[4,512,256]{2,1,0:T(8,128)} %t_ref.3) | copy-start | bytes 6291460
  20.1 0.7 %copy-start.3 = (f32[4,64]{1,0:T(4,128)S(1)}, f32[4,64]{1,0:T(4,128)}, u32[]{:S(2)}) copy-start(f32[4,64]{1,0:T(4,128)} %tf_ref.1) | copy-start | bytes 3076
  37.0 15.4 %copy-start.1 = (f32[4,512,256]{2,1,0:T(8,128)S(1)}, f32[4,512,256]{2,1,0:T(8,128)}, u32[]{:S(2)}) copy-start(f32[4,512,256]{2,1,0:T(8,128)} %t_ref.3) | copy-start | bytes 6291460
  37.7 14.7 %all-to-all-start.2 = ((f32[8,32,128]{2,1,0:T(8,128)}), f32[8,32,128]{2,1,0:T(8,128)S(1)}, u32[]{:S(2)}, u32[]{:S(2)}) async-start(f32[8,32,128]{2,1,0:T(8,128)} %get-tuple-element.17.own_ref), calls=%async_computation.2 | async-start | bytes 262144 | tf_op jit(solution)/shard_map/all_to_all | solution.py:200

commit v3 on v2

v3 whole, which is shorter than its diff:
```python
import jax
import jax.numpy as jnp
from jax import lax
from jax.experimental import pallas as pl
from jax.experimental.pallas import tpu as pltpu
from jax.sharding import PartitionSpec as P

RANK = 64
F32 = jnp.float32
BF16 = jnp.bfloat16
HIGHEST = lax.Precision.HIGHEST
VMEM = pl.BlockSpec(memory_space=pltpu.VMEM)
PIECE = 128
FETCH = 256
GRAM = 3 * RANK // 8
PLANE_FIRST = 37
SUMS_ORDER = (6, 7, 0, 5, 1, 4, 2, 3)
ROWS_ORDER = (6, 7, 3, 1, 0, 2, 5, 4)


def params(mebibytes):
    return pltpu.CompilerParams(vmem_limit_bytes=mebibytes * 1024 * 1024)


def work(flops):
    return pl.CostEstimate(flops=flops, bytes_accessed=10**7, transcendentals=0)


def split(x):
    high = x.astype(BF16)
    return high, (x - high.astype(F32)).astype(BF16)


def dot(a, b, contract, precision=None):
    return lax.dot_general(
        a, b, (contract, ((), ())), precision=precision, preferred_element_type=F32
    )


def spread_kernel(m_ref, out_ref):
    rows = m_ref.shape[0]
    packed = jnp.concatenate(
        [
            jnp.concatenate([m_ref[i : i + 1, :], m_ref[i + 1 : i + 2, :]], axis=1)
            for i in range(0, rows, 2)
        ],
        axis=0,
    )
    out_ref[...] = jnp.broadcast_to(packed[None], out_ref.shape)


def fetch_kernel(t_hbm, tf_hbm, t_ref, tf_ref, gram_ref, sems, tf_sem):
    small = pltpu.make_async_copy(tf_hbm, tf_ref, tf_sem)
    small.start()
    copies = []
    steps, machines, _ = t_ref.shape
    for k in range(steps):
        for p in range(machines // FETCH):
            rows = pl.ds(p * FETCH, FETCH)
            copies.append(
                pltpu.make_async_copy(t_hbm.at[k, rows, :], t_ref.at[k, rows, :], sems.at[k, p])
            )
            copies[-1].start()
    small.wait()
    tf = tf_ref[...]
    gram_ref[...] = dot(tf, tf, ((0,), (0,)), HIGHEST)
    for copy in copies:
        copy.wait()


def pack_gram(gram):
    half = RANK // 2
    rows = [gram[8 * i : 8 * i + 8] for i in range(RANK // 8)]
    return jnp.concatenate(
        [
            jnp.concatenate(rows[0:2], axis=1),
            jnp.concatenate(rows[2:4], axis=1),
            jnp.concatenate([row[:, half:] for row in rows[4:]], axis=1),
        ],
        axis=0,
    )


def unpack_gram(packed):
    half = RANK // 2
    top = jnp.concatenate(
        [packed[i : i + 8, h : h + RANK] for i in (0, 8) for h in (0, RANK)], axis=0
    )
    corner = jnp.concatenate(
        [packed[16:24, half * i : half * (i + 1)] for i in range(4)], axis=0
    )
    bottom = jnp.concatenate([top[:, half:].T, corner], axis=1)
    return jnp.concatenate([top, bottom], axis=0)


def sums_kernel(t_ref, g_ref, tf_ref, out_ref, m_ref):
    steps, machines, metrics = t_ref.shape
    parts = out_ref.shape[0]
    own = machines // parts
    half = own // 2
    cut = 2 * PLANE_FIRST
    top = metrics // 2 - cut
    for h in range(2):
        lanes = slice(h * RANK, (h + 1) * RANK)
        m_ref[pl.ds(2 * cut + h, top, stride=2), :] = g_ref[:top, lanes]
        m_ref[pl.ds(h, cut, stride=2), :] = g_ref[top:, lanes]
    m = m_ref[...]
    gram = pack_gram(dot(m, m, ((0,), (0,)), HIGHEST))
    acc = jnp.zeros((machines, 2 * RANK), F32)
    for k in range(steps):
        right = jnp.concatenate(split(m * tf_ref[k : k + 1, :]), axis=1)
        high, low = split(t_ref[k])
        acc = acc + (dot(high, right, ((1,), (0,))) + dot(low, right, ((1,), (0,))))
    for i in range(parts):
        c = SUMS_ORDER[i]
        block = acc[c * own : (c + 1) * own]
        sums = block[:, :RANK] + block[:, RANK:]
        out_ref[i, :half, :] = jnp.concatenate([sums[:half], sums[half:]], axis=1)
        out_ref[i, half:, :] = gram


def reduce_kernel(r_ref, own_ref, gram_ref):
    parts, rows, _ = own_ref.shape
    total = r_ref[0]
    for c in range(1, parts):
        total = total + r_ref[c]
    own_ref[...] = jnp.broadcast_to(total[None, :rows], own_ref.shape)
    gram_ref[...] = total[rows:]


def inverse_factor(normal):
    wide = 2 * RANK
    count = RANK // 8
    row_id = lax.broadcasted_iota(jnp.int32, (RANK, RANK), 0)
    col_id = lax.broadcasted_iota(jnp.int32, (RANK, RANK), 1)
    both = jnp.concatenate([normal, (row_id == col_id).astype(F32)], axis=1)
    blocks = [both[8 * b : 8 * b + 8] for b in range(count)]
    sub = lax.broadcasted_iota(jnp.int32, (8, wide), 0)

    def column(x, j):
        return jnp.broadcast_to(x[:, j : j + 1], (8, wide))

    def row(x, i):
        return jnp.broadcast_to(x[i : i + 1, :], (8, wide))

    done = []
    for b in range(count):
        panel = blocks[b]
        columns = [column(panel, 8 * b + t) for t in range(8)]
        entry = {(s, t): row(columns[t], s) for s in range(8) for t in range(s, 8)}
        upper = [row(panel, t) for t in range(8)]
        below = {
            i: [column(blocks[i], 8 * b + t) for t in range(8)] for i in range(b + 1, count)
        }
        rows = panel
        for s in range(0, 8, 2):
            v = s + 1
            a, o, d = entry[s, s], entry[s, v], entry[v, v]
            inverse = 1.0 / (a * d - o * o)
            later = range(s + 2, 8)
            first = {t: (entry[s, t] * d - entry[v, t] * o) * inverse for t in later}
            second = {t: (entry[v, t] * a - entry[s, t] * o) * inverse for t in later}
            upper_first = (upper[s] * d - upper[v] * o) * inverse
            upper_second = (upper[v] * a - upper[s] * o) * inverse
            for t in later:
                for q in range(t, 8):
                    entry[t, q] -= first[t] * entry[s, q] + second[t] * entry[v, q]
                upper[t] = upper[t] - (first[t] * upper[s] + second[t] * upper[v])
            for i, side in below.items():
                blocks[i] = blocks[i] - (side[s] * upper_first + side[v] * upper_second)
                for t in later:
                    side[t] = side[t] - (first[t] * side[s] + second[t] * side[v])
            ratio = o / a
            rows = jnp.where(sub == s, upper[s] * lax.rsqrt(a), rows)
            last = (upper[v] - ratio * upper[s]) * lax.rsqrt(d - o * ratio)
            rows = jnp.where(sub == v, last, rows)
        done.append(rows)
    return jnp.concatenate(done, axis=0)[:, RANK:]


def solve_kernel(gram_ref, own_ref, m_ref, tf_ref, times_ref, w_ref, rows_ref):
    inverse = inverse_factor(unpack_gram(gram_ref[...]) * times_ref[...])
    whole = dot(inverse, inverse, ((0,), (0,)), HIGHEST)
    sums = jnp.concatenate([own_ref[0, :, :RANK], own_ref[0, :, RANK:]], axis=0)
    rows_ref[...] = dot(sums, whole, ((1,), (0,)), HIGHEST)
    high, low = split(whole)
    left = jnp.concatenate([high, low, high, low], axis=1)
    m = m_ref[...]
    for k in range(tf_ref.shape[0]):
        high, low = split(m * tf_ref[k : k + 1, :])
        right = jnp.concatenate([high, high, low, low], axis=1)
        high, low = split(dot(left, right, ((1,), (1,))))
        w_ref[k] = jnp.concatenate([high, high, low, low], axis=0)


def residual_kernel(t_ref, s_ref, w_ref, out_ref, held, sems):
    parts, half, _ = s_ref.shape
    steps, machines, _ = t_ref.shape
    copies = []
    per = PIECE // (2 * half)
    for p in range(machines // PIECE):
        pieces = []
        for c in range(p * per, (p + 1) * per):
            block = s_ref[ROWS_ORDER.index(c)]
            pieces += [block[:, :RANK], block[:, RANK:]]
        high, low = split(jnp.concatenate(pieces, axis=0))
        left = jnp.concatenate([high, low, high, low], axis=1)
        rows = pl.ds(p * PIECE, PIECE)
        for k in range(steps):
            held[k, rows, :] = t_ref[k, rows, :] - dot(left, w_ref[k], ((1,), (0,)))
            copy = pltpu.make_async_copy(
                held.at[k, rows, :], out_ref.at[k, rows, :], sems.at[p, k]
            )
            copy.start()
            copies.append(copy)
    for copy in copies:
        copy.wait()


def local(parts, plane, tensor, metric_factor, time_factor):
    steps, machines, metrics = tensor.shape
    own = machines // parts
    rows = metric_factor.shape[0]
    plane_order = [[(i + PLANE_FIRST) % plane for i in range(plane)]]
    copies = pl.pallas_call(
        spread_kernel,
        out_shape=jax.ShapeDtypeStruct((plane, rows // 2, 2 * RANK), F32),
        in_specs=[VMEM],
        out_specs=VMEM,
        compiler_params=params(2),
    )(metric_factor)
    gathered = lax.all_to_all(copies, "mach", 0, 0, axis_index_groups=plane_order).reshape(metrics // 2, 2 * RANK)
    held, times, time_gram = pl.pallas_call(
        fetch_kernel,
        out_shape=(
            jax.ShapeDtypeStruct(tensor.shape, F32),
            jax.ShapeDtypeStruct(time_factor.shape, F32),
            jax.ShapeDtypeStruct((RANK, RANK), F32),
        ),
        in_specs=[pl.BlockSpec(memory_space=pltpu.HBM)] * 2,
        out_specs=(VMEM,) * 3,
        scratch_shapes=[
            pltpu.SemaphoreType.DMA((steps, machines // FETCH)),
            pltpu.SemaphoreType.DMA,
        ],
        compiler_params=params(12),
        cost_estimate=work(10**9),
    )(
        pltpu.with_memory_space_constraint(tensor, pltpu.HBM),
        pltpu.with_memory_space_constraint(time_factor, pltpu.HBM),
    )
    half = own // 2
    partial, metric_block = pl.pallas_call(
        sums_kernel,
        out_shape=(
            jax.ShapeDtypeStruct((parts, half + GRAM, 2 * RANK), F32),
            jax.ShapeDtypeStruct((metrics, RANK), F32),
        ),
        in_specs=[VMEM] * 3,
        out_specs=(VMEM, VMEM),
        compiler_params=params(12),
    )(held, gathered, times)
    received = lax.all_to_all(partial, "met", 0, 0, axis_index_groups=[SUMS_ORDER])
    own_sums, gram = pl.pallas_call(
        reduce_kernel,
        out_shape=(
            jax.ShapeDtypeStruct((parts, half, 2 * RANK), F32),
            jax.ShapeDtypeStruct((GRAM, 2 * RANK), F32),
        ),
        in_specs=[VMEM],
        out_specs=(VMEM, VMEM),
        compiler_params=params(4),
    )(received)
    sums = lax.all_to_all(own_sums, "met", 0, 0, axis_index_groups=[ROWS_ORDER])
    weights, own_rows = pl.pallas_call(
        solve_kernel,
        out_shape=(
            jax.ShapeDtypeStruct((steps, 4 * RANK, metrics), BF16),
            jax.ShapeDtypeStruct((own, RANK), F32),
        ),
        in_specs=[VMEM] * 5,
        out_specs=(VMEM, VMEM),
        compiler_params=params(8),
        cost_estimate=work(10**9),
    )(gram, own_sums, metric_block, times, time_gram)
    residual = pl.pallas_call(
        residual_kernel,
        out_shape=jax.ShapeDtypeStruct(tensor.shape, F32),
        in_specs=[VMEM] * 3,
        out_specs=pl.BlockSpec(memory_space=pl.ANY),
        scratch_shapes=[
            pltpu.VMEM(tensor.shape, F32),
            pltpu.SemaphoreType.DMA((machines // PIECE, steps)),
        ],
        compiler_params=params(12),
    )(held, sums, weights)
    return own_rows, residual


def solution(mesh):
    def run(tensor, metric_factor, time_factor):
        return local(mesh.shape["met"], mesh.shape["mach"], tensor, metric_factor, time_factor)

    return jax.shard_map(
        run,
        mesh=mesh,
        in_specs=(P(None, "mach", "met"), P(("met", "mach"), None), P()),
        out_specs=(P(("mach", "met"), None), P(None, "mach", "met")),
        check_vma=False,
    )
```

time: 54.8 us -> 50.8 us (0.927)
  the two profiles are of different devices: /device:TPU:1 before, /device:TPU:4 now
where the time goes in v3:
time: 50.8 us; the launch traced here: 50.5 us
  starting transfers between devices  18.9 us (37%)
  blocking collectives  15.5 us (31%)
  Pallas kernels  9.75 us (19%)
  waiting for transfers between devices  4.96 us (10%)
  local copies, waits for them, and re-layouts  0.67 us (1%)
  between operations  0.66 us (1%)
    all_to_all x1, blocking collectives, local(): lax.all_to_all(partial, 'met', 0, 0, axis_index_groups=[SUMS_ORDER])  15.5 us
    all_to_all x1, starting transfers between devices, local(): lax.all_to_all(copies, 'mach', 0, 0, axis_index_groups=plane_order)  12.9 us
    all_to_all x1, starting transfers between devices, local(): sums = lax.all_to_all(own_sums, 'met', 0, 0, axis_index_groups=[ROWS_ORDER])  6.02 us
    pallas_call x1, Pallas kernels, local(): pl.pallas_call(solve_kernel, out_shape=(jax.ShapeDtypeStruct((steps, 4 *...  3.93 us
    all_to_all x1, waiting for transfers between devices, local(): lax.all_to_all(copies, 'mach', 0, 0, axis_index_groups=plane_order)  3.56 us
    pallas_call x1, Pallas kernels, local(): pl.pallas_call(residual_kernel, out_shape=jax.ShapeDtypeStruct(tensor.sha...  1.76 us
    pallas_call x1, Pallas kernels, local(): pl.pallas_call(fetch_kernel, out_shape=(jax.ShapeDtypeStruct(tensor.shape...  1.6 us
    all_to_all x1, waiting for transfers between devices, local(): sums = lax.all_to_all(own_sums, 'met', 0, 0, axis_index_groups=[ROWS_ORDER])  1.39 us
  transfers between devices with their start and end apart: 2, of which 2 were waited for; matrix products, arithmetic and copies ran while one was open for 0% of the time, Pallas kernels for 11%

profile of v3, /device:TPU:4, one launch (start us, length us, event | category | flops | bytes accessed | tf_op | source)
XLA Modules:
  0.0 50.5 jit_solution(11711121317858141677)
XLA Ops:
  0.6 0.0 copy-start
  0.6 0.7 %copy-done = f32[4,64]{1,0:T(4,128)S(1)} copy-done((f32[4,64]{1,0:T(4,128)S(1)}, f32[4,64]{1,0:T(4,128)}, u32[]{:S(2)}) %copy-start) | copy-done | bytes 1048
  1.3 0.7 %shard_map.51 = f32[64,2,128]{2,1,0:T(2,128)} custom-call(f32[4,64]{1,0:T(4,128)S(1)} %copy-done), custom_call_target="tpu_custom_call" | custom-call | tf_op jit(solution)/shard_map/pallas_call | solution.py:225
  2.0 12.9 %all-to-all-start = ((f32[64,2,128]{2,1,0:T(2,128)}), f32[64,2,128]{2,1,0:T(2,128)S(1)}, u32[]{:S(2)}, u32[]{:S(2)}) async-start(f32[64,2,128]{2,1,0:T(2,128)} %shard_map.51), calls=%async_computation | async-start | bytes 131072 | tf_op jit(solution)/shard_map/all_to_all | solution.py:232
  14.9 1.6 %shard_map.50 = (f32[4,512,256]{2,1,0:T(8,128)S(1)}, f32[4,64]{1,0:T(4,128)S(1)}, f32[64,64]{1,0:T(8,128)S(1)}) custom-call(f32[4,512,256]{2,1,0:T(8,128)} %t_hbm.1, f32[4,64]{1,0:T(4,128)} %tf_hbm.1), custom_call_target="tpu_custom_call" | custom-call | flops 1000000000 | bytes 10000000 | tf_op jit(solution)/shard_map/pallas_call | solution.py:233
  16.5 3.6 %all-to-all-done = f32[64,2,128]{2,1,0:T(2,128)S(1)} async-done(((f32[64,2,128]{2,1,0:T(2,128)}), f32[64,2,128]{2,1,0:T(2,128)S(1)}, u32[]{:S(2)}, u32[]{:S(2)}) %all-to-all-start) | async-done | bytes 65568 | tf_op jit(solution)/shard_map/all_to_all | solution.py:232
  20.1 1.1 %shard_map.52 = (f32[8,56,128]{2,1,0:T(8,128)S(1)}, f32[256,64]{1,0:T(8,128)S(1)}) custom-call(f32[4,512,256]{2,1,0:T(8,128)S(1)} %get-tuple-element.11.t_ref, f32[128,128]{1,0:T(8,128)S(1)} %bitcast.1, f32[4,64]{1,0:T(4,128)S(1)} %get-tuple-element.12.tf_ref), custom_call_target="tpu_custom_call" | custom-call | tf_op jit(solution)/shard_map/pallas_call | solution.py:253
  21.2 15.5 %all_to_all.15.r_ref = f32[8,56,128]{2,1,0:T(8,128)S(1)} all-to-all(f32[8,56,128]{2,1,0:T(8,128)S(1)} %get-tuple-element.13), channel_id=1, replica_groups={{384,448,0,320,64,256,128,192},{385,449,1,321,65,257,129,193},{386,450,..., dimensions={0} | all-to-all | bytes 458752 | tf_op jit(solution)/shard_map/all_to_all | solution.py:263
  36.7 0.7 %shard_map.53 = (f32[8,32,128]{2,1,0:T(8,128)}, f32[24,128]{1,0:T(8,128)S(1)}) custom-call(f32[8,56,128]{2,1,0:T(8,128)S(1)} %all_to_all.15.r_ref), custom_call_target="tpu_custom_call" | custom-call | tf_op jit(solution)/shard_map/pallas_call | solution.py:264
  37.4 6.0 %all-to-all-start.2 = ((f32[8,32,128]{2,1,0:T(8,128)}), f32[8,32,128]{2,1,0:T(8,128)S(1)}, u32[]{:S(2)}, u32[]{:S(2)}) async-start(f32[8,32,128]{2,1,0:T(8,128)} %get-tuple-element.15.own_ref), calls=%async_computation.2 | async-start | bytes 262144 | tf_op jit(solution)/shard_map/all_to_all | solution.py:274
  43.4 3.9 %shard_map.54 = (bf16[4,256,256]{2,1,0:T(8,128)(2,1)S(1)}, f32[64,64]{1,0:T(8,128)}) custom-call(f32[24,128]{1,0:T(8,128)S(1)} %get-tuple-element.14.gram_ref, f32[8,32,128]{2,1,0:T(8,128)} %get-tuple-element.15.own_ref, f32[256,64]{1,0:T(8,128)S(1)} %get-tuple-element.16.m_ref, f32[4,64]{1,0:T(4,128)S(1)} %get-tuple-element.12.tf_ref, ...), custom_call_target="tpu_custom_call" | custom-call | flops 1000000000 | bytes 10000000 | tf_op jit(solution)/shard_map/pallas_call | solution.py:275
  47.3 1.4 %all-to-all-done.2.s_ref = f32[8,32,128]{2,1,0:T(8,128)S(1)} async-done(((f32[8,32,128]{2,1,0:T(8,128)}), f32[8,32,128]{2,1,0:T(8,128)S(1)}, u32[]{:S(2)}, u32[]{:S(2)}) %all-to-all-start.2) | async-done | bytes 131104 | tf_op jit(solution)/shard_map/all_to_all | solution.py:274
  48.7 1.8 %shard_map.55 = f32[4,512,256]{2,1,0:T(8,128)} custom-call(f32[4,512,256]{2,1,0:T(8,128)S(1)} %get-tuple-element.11.t_ref, f32[8,32,128]{2,1,0:T(8,128)S(1)} %all-to-all-done.2.s_ref, bf16[4,256,256]{2,1,0:T(8,128)(2,1)S(1)} %get-tuple-element.19.w_ref), custom_call_target="tpu_custom_call" | custom-call | tf_op jit(solution)/shard_map/pallas_call | solution.py:286
Async XLA Ops:
  0.6 0.7 %copy-start = (f32[4,64]{1,0:T(4,128)S(1)}, f32[4,64]{1,0:T(4,128)}, u32[]{:S(2)}) copy-start(f32[4,64]{1,0:T(4,128)} %m_ref.1) | copy-start | bytes 3076
  2.0 18.1 %all-to-all-start = ((f32[64,2,128]{2,1,0:T(2,128)}), f32[64,2,128]{2,1,0:T(2,128)S(1)}, u32[]{:S(2)}, u32[]{:S(2)}) async-start(f32[64,2,128]{2,1,0:T(2,128)} %shard_map.51), calls=%async_computation | async-start | bytes 131072 | tf_op jit(solution)/shard_map/all_to_all | solution.py:232
  37.4 11.3 %all-to-all-start.2 = ((f32[8,32,128]{2,1,0:T(8,128)}), f32[8,32,128]{2,1,0:T(8,128)S(1)}, u32[]{:S(2)}, u32[]{:S(2)}) async-start(f32[8,32,128]{2,1,0:T(8,128)} %get-tuple-element.15.own_ref), calls=%async_computation.2 | async-start | bytes 262144 | tf_op jit(solution)/shard_map/all_to_all | solution.py:274

commit v4 on v3

--- a/solution.py
+++ b/solution.py
@@ -37,19 +37,9 @@
     )
 
 
-def spread_kernel(m_ref, out_ref):
-    rows = m_ref.shape[0]
-    packed = jnp.concatenate(
-        [
-            jnp.concatenate([m_ref[i : i + 1, :], m_ref[i + 1 : i + 2, :]], axis=1)
-            for i in range(0, rows, 2)
-        ],
-        axis=0,
-    )
-    out_ref[...] = jnp.broadcast_to(packed[None], out_ref.shape)
-
-
-def fetch_kernel(t_hbm, tf_hbm, t_ref, tf_ref, gram_ref, sems, tf_sem):
+def begin_kernel(m_hbm, t_hbm, tf_hbm, out_ref, t_ref, tf_ref, gram_ref, m_ref, sems, m_sem, tf_sem):
+    first = pltpu.make_async_copy(m_hbm, m_ref, m_sem)
+    first.start()
     small = pltpu.make_async_copy(tf_hbm, tf_ref, tf_sem)
     small.start()
     copies = []
@@ -61,6 +51,15 @@
                 pltpu.make_async_copy(t_hbm.at[k, rows, :], t_ref.at[k, rows, :], sems.at[k, p])
             )
             copies[-1].start()
+    first.wait()
+    packed = jnp.concatenate(
+        [
+            jnp.concatenate([m_ref[i : i + 1, :], m_ref[i + 1 : i + 2, :]], axis=1)
+            for i in range(0, m_ref.shape[0], 2)
+        ],
+        axis=0,
+    )
+    out_ref[...] = jnp.broadcast_to(packed[None], out_ref.shape)
     small.wait()
     tf = tf_ref[...]
     gram_ref[...] = dot(tf, tf, ((0,), (0,)), HIGHEST)
@@ -222,32 +221,30 @@
     own = machines // parts
     rows = metric_factor.shape[0]
     plane_order = [[(i + PLANE_FIRST) % plane for i in range(plane)]]
-    copies = pl.pallas_call(
-        spread_kernel,
-        out_shape=jax.ShapeDtypeStruct((plane, rows // 2, 2 * RANK), F32),
-        in_specs=[VMEM],
-        out_specs=VMEM,
-        compiler_params=params(2),
-    )(metric_factor)
-    gathered = lax.all_to_all(copies, "mach", 0, 0, axis_index_groups=plane_order).reshape(metrics // 2, 2 * RANK)
-    held, times, time_gram = pl.pallas_call(
-        fetch_kernel,
+    copies, held, times, time_gram = pl.pallas_call(
+        begin_kernel,
         out_shape=(
+            jax.ShapeDtypeStruct((plane, rows // 2, 2 * RANK), F32),
             jax.ShapeDtypeStruct(tensor.shape, F32),
             jax.ShapeDtypeStruct(time_factor.shape, F32),
             jax.ShapeDtypeStruct((RANK, RANK), F32),
         ),
-        in_specs=[pl.BlockSpec(memory_space=pltpu.HBM)] * 2,
-        out_specs=(VMEM,) * 3,
+        in_specs=[pl.BlockSpec(memory_space=pltpu.HBM)] * 3,
+        out_specs=(VMEM,) * 4,
         scratch_shapes=[
+            pltpu.VMEM(metric_factor.shape, F32),
             pltpu.SemaphoreType.DMA((steps, machines // FETCH)),
+            pltpu.SemaphoreType.DMA,
             pltpu.SemaphoreType.DMA,
         ],
         compiler_params=params(12),
-        cost_estimate=work(10**9),
     )(
+        pltpu.with_memory_space_constraint(metric_factor, pltpu.HBM),
         pltpu.with_memory_space_constraint(tensor, pltpu.HBM),
         pltpu.with_memory_space_constraint(time_factor, pltpu.HBM),
+    )
+    gathered = lax.all_to_all(copies, "mach", 0, 0, axis_index_groups=plane_order).reshape(
+        metrics // 2, 2 * RANK
     )
     half = own // 2
     partial, metric_block = pl.pallas_call(

time: 50.8 us -> 50.3 us (level)
  blocking collectives: 15.5 us -> 32.4 us
  starting transfers between devices: 18.9 us -> 6.46 us
  waiting for transfers between devices: 4.96 us -> 1.39 us
  local copies, waits for them, and re-layouts: 0.67 us -> 0 us
  Pallas kernels: 9.75 us -> 9.08 us
    all_to_all x0 -> x1, blocking collectives: none -> 17.9 us  [local(): lax.all_to_all(copies, 'mach', 0, 0, axis_index_groups=plane_order)]
    all_to_all x1 -> x0, starting transfers between devices: 12.9 us -> none  [local(): lax.all_to_all(copies, 'mach', 0, 0, axis_index_groups=plane_order)]
    all_to_all x1 -> x0, waiting for transfers between devices: 3.56 us -> none  [local(): lax.all_to_all(copies, 'mach', 0, 0, axis_index_groups=plane_order)]
    all_to_all x1, blocking collectives: 15.5 us -> 14.6 us  [local(): lax.all_to_all(partial, 'met', 0, 0, axis_index_groups=[SUMS_ORDER])]
    unnamed x2 -> x0, local copies, waits for them, and re-layouts: 0.67 us -> none
    pallas_call x2 -> x1, Pallas kernels: 2.32 us -> 1.65 us  [local(): pl.pallas_call(begin_kernel, out_shape=(jax.ShapeDtypeStruct((plane, rows...]
  transfers between devices with their start and end apart: 2 -> 1, of which waited for: 2 -> 1; matrix products, arithmetic and copies ran while one was open for 0% -> 0% of each run, Pallas kernels for 11% -> 8%
where the time goes in v4:
time: 50.3 us; the launch traced here: 50 us
  blocking collectives  32.4 us (64%)
  Pallas kernels  9.08 us (18%)
  starting transfers between devices  6.46 us (13%)
  waiting for transfers between devices  1.39 us (3%)
  between operations  0.64 us (1%)
    all_to_all x1, blocking collectives, local(): lax.all_to_all(copies, 'mach', 0, 0, axis_index_groups=plane_order)  17.9 us
    all_to_all x1, blocking collectives, local(): lax.all_to_all(partial, 'met', 0, 0, axis_index_groups=[SUMS_ORDER])  14.6 us
    all_to_all x1, starting transfers between devices, local(): sums = lax.all_to_all(own_sums, 'met', 0, 0, axis_index_groups=[ROWS_ORDER])  6.46 us
    pallas_call x1, Pallas kernels, local(): pl.pallas_call(solve_kernel, out_shape=(jax.ShapeDtypeStruct((steps, 4 *...  3.93 us
    pallas_call x1, Pallas kernels, local(): pl.pallas_call(residual_kernel, out_shape=jax.ShapeDtypeStruct(tensor.sha...  1.76 us
    pallas_call x1, Pallas kernels, local(): pl.pallas_call(begin_kernel, out_shape=(jax.ShapeDtypeStruct((plane, rows...  1.65 us
    all_to_all x1, waiting for transfers between devices, local(): sums = lax.all_to_all(own_sums, 'met', 0, 0, axis_index_groups=[ROWS_ORDER])  1.39 us
    pallas_call x1, Pallas kernels, local(): pl.pallas_call(sums_kernel, out_shape=(jax.ShapeDtypeStruct((parts, half...  1.07 us
  transfers between devices with their start and end apart: 1, of which 1 were waited for; matrix products, arithmetic and copies ran while one was open for 0% of the time, Pallas kernels for 8%

profile of v4, /device:TPU:4, one launch (start us, length us, event | category | flops | bytes accessed | tf_op | source)
XLA Modules:
  0.0 50.0 jit_solution(5364905370639113856)
XLA Ops:
  0.6 1.6 %shard_map.50 = (f32[64,2,128]{2,1,0:T(2,128)S(1)}, f32[4,512,256]{2,1,0:T(8,128)S(1)}, f32[4,64]{1,0:T(4,128)S(1)}, f32[64,64]{1,0:T(8,128)S(1)}) custom-call(f32[4,64]{1,0:T(4,128)} %m_hbm.1, f32[4,512,256]{2,1,0:T(8,128)} %t_hbm.1, f32[4,64]{1,0:T(4,128)} %tf_hbm.1), custom_call_target="tpu_custom_call" | custom-call | tf_op jit(solution)/shard_map/pallas_call | solution.py:224
  2.3 17.9 %all_to_all.15 = f32[64,2,128]{2,1,0:T(2,128)S(1)} all-to-all(f32[64,2,128]{2,1,0:T(2,128)S(1)} %get-tuple-element.13), channel_id=1, replica_groups={{37,38,39,40,41,42,43,44,45,46,47,48,49,50,51,52,53,54,55,56,57,58,59,6..., dimensions={0} | all-to-all | bytes 131072 | tf_op jit(solution)/shard_map/all_to_all | solution.py:246
  20.2 1.1 %shard_map.51 = (f32[8,56,128]{2,1,0:T(8,128)S(1)}, f32[256,64]{1,0:T(8,128)S(1)}) custom-call(f32[4,512,256]{2,1,0:T(8,128)S(1)} %get-tuple-element.12.t_ref, f32[128,128]{1,0:T(8,128)S(1)} %bitcast.1, f32[4,64]{1,0:T(4,128)S(1)} %get-tuple-element.14.tf_ref), custom_call_target="tpu_custom_call" | custom-call | tf_op jit(solution)/shard_map/pallas_call | solution.py:250
  21.2 14.6 %all_to_all.16.r_ref = f32[8,56,128]{2,1,0:T(8,128)S(1)} all-to-all(f32[8,56,128]{2,1,0:T(8,128)S(1)} %get-tuple-element.15), channel_id=1, replica_groups={{384,448,0,320,64,256,128,192},{385,449,1,321,65,257,129,193},{386,450,..., dimensions={0} | all-to-all | bytes 458752 | tf_op jit(solution)/shard_map/all_to_all | solution.py:260
  35.8 0.7 %shard_map.52 = (f32[8,32,128]{2,1,0:T(8,128)}, f32[24,128]{1,0:T(8,128)S(1)}) custom-call(f32[8,56,128]{2,1,0:T(8,128)S(1)} %all_to_all.16.r_ref), custom_call_target="tpu_custom_call" | custom-call | tf_op jit(solution)/shard_map/pallas_call | solution.py:261
  36.5 6.5 %all-to-all-start.2 = ((f32[8,32,128]{2,1,0:T(8,128)}), f32[8,32,128]{2,1,0:T(8,128)S(1)}, u32[]{:S(2)}, u32[]{:S(2)}) async-start(f32[8,32,128]{2,1,0:T(8,128)} %get-tuple-element.17.own_ref), calls=%async_computation.2 | async-start | bytes 262144 | tf_op jit(solution)/shard_map/all_to_all | solution.py:271
  42.9 3.9 %shard_map.53 = (bf16[4,256,256]{2,1,0:T(8,128)(2,1)S(1)}, f32[64,64]{1,0:T(8,128)}) custom-call(f32[24,128]{1,0:T(8,128)S(1)} %get-tuple-element.16.gram_ref, f32[8,32,128]{2,1,0:T(8,128)} %get-tuple-element.17.own_ref, f32[256,64]{1,0:T(8,128)S(1)} %get-tuple-element.18.m_ref, f32[4,64]{1,0:T(4,128)S(1)} %get-tuple-element.14.tf_ref, ...), custom_call_target="tpu_custom_call" | custom-call | flops 1000000000 | bytes 10000000 | tf_op jit(solution)/shard_map/pallas_call | solution.py:272
  46.9 1.4 %all-to-all-done.2.s_ref = f32[8,32,128]{2,1,0:T(8,128)S(1)} async-done(((f32[8,32,128]{2,1,0:T(8,128)}), f32[8,32,128]{2,1,0:T(8,128)S(1)}, u32[]{:S(2)}, u32[]{:S(2)}) %all-to-all-start.2) | async-done | bytes 131104 | tf_op jit(solution)/shard_map/all_to_all | solution.py:271
  48.3 1.8 %shard_map.54 = f32[4,512,256]{2,1,0:T(8,128)} custom-call(f32[4,512,256]{2,1,0:T(8,128)S(1)} %get-tuple-element.12.t_ref, f32[8,32,128]{2,1,0:T(8,128)S(1)} %all-to-all-done.2.s_ref, bf16[4,256,256]{2,1,0:T(8,128)(2,1)S(1)} %get-tuple-element.21.w_ref), custom_call_target="tpu_custom_call" | custom-call | tf_op jit(solution)/shard_map/pallas_call | solution.py:283
Async XLA Ops:
  36.5 11.8 %all-to-all-start.2 = ((f32[8,32,128]{2,1,0:T(8,128)}), f32[8,32,128]{2,1,0:T(8,128)S(1)}, u32[]{:S(2)}, u32[]{:S(2)}) async-start(f32[8,32,128]{2,1,0:T(8,128)} %get-tuple-element.17.own_ref), calls=%async_computation.2 | async-start | bytes 262144 | tf_op jit(solution)/shard_map/all_to_all | solution.py:271

commit v5 on v4

--- a/solution.py
+++ b/solution.py
@@ -14,7 +14,7 @@
 FETCH = 256
 GRAM = 3 * RANK // 8
 PLANE_FIRST = 37
-SUMS_ORDER = (6, 7, 0, 5, 1, 4, 2, 3)
+SUMS_ORDER = (6, 7, 2, 3, 5, 0, 1, 4)
 ROWS_ORDER = (6, 7, 3, 1, 0, 2, 5, 4)
 
 
@@ -99,22 +99,30 @@
     half = own // 2
     cut = 2 * PLANE_FIRST
     top = metrics // 2 - cut
-    for h in range(2):
-        lanes = slice(h * RANK, (h + 1) * RANK)
-        m_ref[pl.ds(2 * cut + h, top, stride=2), :] = g_ref[:top, lanes]
-        m_ref[pl.ds(h, cut, stride=2), :] = g_ref[top:, lanes]
+    pairs = g_ref[...]
+    swapped = pltpu.roll(pairs, RANK, 1)
+    left = lax.broadcasted_iota(jnp.int32, pairs.shape, 1) < RANK
+    for h, rows in enumerate((jnp.where(left, pairs, swapped), jnp.where(left, swapped, pairs))):
+        m_ref[pl.ds(2 * cut + h, top, stride=2), :] = rows[:top]
+        m_ref[pl.ds(h, cut, stride=2), :] = rows[top:]
     m = m_ref[...]
-    gram = pack_gram(dot(m, m, ((0,), (0,)), HIGHEST))
-    acc = jnp.zeros((machines, 2 * RANK), F32)
+    left = lax.broadcasted_iota(jnp.int32, m.shape, 1) < RANK
+    factors = jnp.concatenate([tf_ref[...], tf_ref[...]], axis=1)
+    acc = None
     for k in range(steps):
-        right = jnp.concatenate(split(m * tf_ref[k : k + 1, :]), axis=1)
+        high, low = split(m * factors[k : k + 1, :])
+        right = jnp.where(left, high.astype(F32), low.astype(F32)).astype(BF16)
         high, low = split(t_ref[k])
-        acc = acc + (dot(high, right, ((1,), (0,))) + dot(low, right, ((1,), (0,))))
+        term = dot(high, right, ((1,), (0,))) + dot(low, right, ((1,), (0,)))
+        acc = term if acc is None else acc + term
+    once = m[:, :RANK]
+    gram = pack_gram(dot(once, once, ((0,), (0,)), HIGHEST))
+    left = lax.broadcasted_iota(jnp.int32, (half, 2 * RANK), 1) < RANK
     for i in range(parts):
         c = SUMS_ORDER[i]
         block = acc[c * own : (c + 1) * own]
-        sums = block[:, :RANK] + block[:, RANK:]
-        out_ref[i, :half, :] = jnp.concatenate([sums[:half], sums[half:]], axis=1)
+        sums = block + pltpu.roll(block, RANK, 1)
+        out_ref[i, :half, :] = jnp.where(left, sums[:half], sums[half:])
         out_ref[i, half:, :] = gram
 
 
@@ -185,9 +193,9 @@
     high, low = split(whole)
     left = jnp.concatenate([high, low, high, low], axis=1)
     m = m_ref[...]
+    factors = jnp.concatenate([tf_ref[...], tf_ref[...]], axis=1)
     for k in range(tf_ref.shape[0]):
-        high, low = split(m * tf_ref[k : k + 1, :])
-        right = jnp.concatenate([high, high, low, low], axis=1)
+        right = jnp.concatenate(split(m * factors[k : k + 1, :]), axis=1)
         high, low = split(dot(left, right, ((1,), (1,))))
         w_ref[k] = jnp.concatenate([high, high, low, low], axis=0)
 
@@ -251,7 +259,7 @@
         sums_kernel,
         out_shape=(
             jax.ShapeDtypeStruct((parts, half + GRAM, 2 * RANK), F32),
-            jax.ShapeDtypeStruct((metrics, RANK), F32),
+            jax.ShapeDtypeStruct((metrics, 2 * RANK), F32),
         ),
         in_specs=[VMEM] * 3,
         out_specs=(VMEM, VMEM),

time: 50.3 us -> 50 us (level)
  the two profiles are of different devices: /device:TPU:4 before, /device:TPU:1 now
where the time goes in v5:
time: 50 us; the launch traced here: 49.1 us
  blocking collectives  32.7 us (65%)
  Pallas kernels  8.94 us (18%)
  starting transfers between devices  6.42 us (13%)
  between operations  0.65 us (1%)
    all_to_all x1, blocking collectives, local(): lax.all_to_all(copies, 'mach', 0, 0, axis_index_groups=plane_order)  19.1 us
    all_to_all x1, blocking collectives, local(): lax.all_to_all(partial, 'met', 0, 0, axis_index_groups=[SUMS_ORDER])  13.6 us
    all_to_all x1, starting transfers between devices, local(): sums = lax.all_to_all(own_sums, 'met', 0, 0, axis_index_groups=[ROWS_ORDER])  6.42 us
    pallas_call x1, Pallas kernels, local(): pl.pallas_call(solve_kernel, out_shape=(jax.ShapeDtypeStruct((steps, 4 *...  3.92 us
    pallas_call x1, Pallas kernels, local(): pl.pallas_call(residual_kernel, out_shape=jax.ShapeDtypeStruct(tensor.sha...  1.76 us
    pallas_call x1, Pallas kernels, local(): pl.pallas_call(begin_kernel, out_shape=(jax.ShapeDtypeStruct((plane, rows...  1.65 us
  transfers between devices with their start and end apart: 1, of which 1 were waited for; matrix products, arithmetic and copies ran while one was open for 0% of the time, Pallas kernels for 8%

profile of v5, /device:TPU:1, one launch (start us, length us, event | category | flops | bytes accessed | tf_op | source)
XLA Modules:
  0.0 49.1 jit_solution(12552833832778710877)
XLA Ops:
  0.6 1.6 %shard_map.50 = (f32[64,2,128]{2,1,0:T(2,128)S(1)}, f32[4,512,256]{2,1,0:T(8,128)S(1)}, f32[4,64]{1,0:T(4,128)S(1)}, f32[64,64]{1,0:T(8,128)S(1)}) custom-call(f32[4,64]{1,0:T(4,128)} %m_hbm.1, f32[4,512,256]{2,1,0:T(8,128)} %t_hbm.1, f32[4,64]{1,0:T(4,128)} %tf_hbm.1), custom_call_target="tpu_custom_call" | custom-call | tf_op jit(solution)/shard_map/pallas_call | solution.py:232
  2.3 19.1 %all_to_all.15 = f32[64,2,128]{2,1,0:T(2,128)S(1)} all-to-all(f32[64,2,128]{2,1,0:T(2,128)S(1)} %get-tuple-element.13), channel_id=1, replica_groups={{37,38,39,40,41,42,43,44,45,46,47,48,49,50,51,52,53,54,55,56,57,58,59,6..., dimensions={0} | all-to-all | bytes 131072 | tf_op jit(solution)/shard_map/all_to_all | solution.py:254
  21.4 0.9 %shard_map.51 = (f32[8,56,128]{2,1,0:T(8,128)S(1)}, f32[256,128]{1,0:T(8,128)S(1)}) custom-call(f32[4,512,256]{2,1,0:T(8,128)S(1)} %get-tuple-element.12.t_ref, f32[128,128]{1,0:T(8,128)S(1)} %bitcast.1, f32[4,64]{1,0:T(4,128)S(1)} %get-tuple-element.14.tf_ref), custom_call_target="tpu_custom_call" | custom-call | tf_op jit(solution)/shard_map/pallas_call | solution.py:258
  22.3 13.6 %all_to_all.16.r_ref = f32[8,56,128]{2,1,0:T(8,128)S(1)} all-to-all(f32[8,56,128]{2,1,0:T(8,128)S(1)} %get-tuple-element.15), channel_id=1, replica_groups={{384,448,128,192,320,0,64,256},{385,449,129,193,321,1,65,257},{386,450,..., dimensions={0} | all-to-all | bytes 458752 | tf_op jit(solution)/shard_map/all_to_all | solution.py:268
  35.9 0.7 %shard_map.52 = (f32[8,32,128]{2,1,0:T(8,128)}, f32[24,128]{1,0:T(8,128)S(1)}) custom-call(f32[8,56,128]{2,1,0:T(8,128)S(1)} %all_to_all.16.r_ref), custom_call_target="tpu_custom_call" | custom-call | tf_op jit(solution)/shard_map/pallas_call | solution.py:269
  36.6 6.4 %all-to-all-start.2 = ((f32[8,32,128]{2,1,0:T(8,128)}), f32[8,32,128]{2,1,0:T(8,128)S(1)}, u32[]{:S(2)}, u32[]{:S(2)}) async-start(f32[8,32,128]{2,1,0:T(8,128)} %get-tuple-element.17.own_ref), calls=%async_computation.2 | async-start | bytes 262144 | tf_op jit(solution)/shard_map/all_to_all | solution.py:279
  43.0 3.9 %shard_map.53 = (bf16[4,256,256]{2,1,0:T(8,128)(2,1)S(1)}, f32[64,64]{1,0:T(8,128)}) custom-call(f32[24,128]{1,0:T(8,128)S(1)} %get-tuple-element.16.gram_ref, f32[8,32,128]{2,1,0:T(8,128)} %get-tuple-element.17.own_ref, f32[256,128]{1,0:T(8,128)S(1)} %get-tuple-element.18.m_ref, f32[4,64]{1,0:T(4,128)S(1)} %get-tuple-element.14.tf_ref, ...), custom_call_target="tpu_custom_call" | custom-call | flops 1000000000 | bytes 10000000 | tf_op jit(solution)/shard_map/pallas_call | solution.py:280
  46.9 0.5 all-to-all-done.2.s_ref
  47.4 1.8 %shard_map.54 = f32[4,512,256]{2,1,0:T(8,128)} custom-call(f32[4,512,256]{2,1,0:T(8,128)S(1)} %get-tuple-element.12.t_ref, f32[8,32,128]{2,1,0:T(8,128)S(1)} %all-to-all-done.2.s_ref, bf16[4,256,256]{2,1,0:T(8,128)(2,1)S(1)} %get-tuple-element.21.w_ref), custom_call_target="tpu_custom_call" | custom-call | tf_op jit(solution)/shard_map/pallas_call | solution.py:291
Async XLA Ops:
  36.6 10.8 %all-to-all-start.2 = ((f32[8,32,128]{2,1,0:T(8,128)}), f32[8,32,128]{2,1,0:T(8,128)S(1)}, u32[]{:S(2)}, u32[]{:S(2)}) async-start(f32[8,32,128]{2,1,0:T(8,128)} %get-tuple-element.17.own_ref), calls=%async_computation.2 | async-start | bytes 262144 | tf_op jit(solution)/shard_map/all_to_all | solution.py:279

commit v6 on v5

--- a/solution.py
+++ b/solution.py
@@ -14,8 +14,8 @@
 FETCH = 256
 GRAM = 3 * RANK // 8
 PLANE_FIRST = 37
-SUMS_ORDER = (6, 7, 2, 3, 5, 0, 1, 4)
-ROWS_ORDER = (6, 7, 3, 1, 0, 2, 5, 4)
+SUMS_ORDER = (6, 2, 7, 3, 5, 0, 1, 4)
+ROWS_ORDER = (6, 7, 3, 5, 0, 2, 1, 4)
 
 
 def params(mebibytes):

time: 50 us -> 49.9 us (level); the launches traced: 49.1 us -> 49.6 us
  blocking collectives: 32.7 us -> 34.5 us
  starting transfers between devices: 6.42 us -> 4.85 us
    all_to_all x1, blocking collectives: 13.6 us -> 15.4 us  [local(): lax.all_to_all(partial, 'met', 0, 0, axis_index_groups=[SUMS_ORDER])]
    all_to_all x1, starting transfers between devices: 6.42 us -> 4.85 us  [local(): sums = lax.all_to_all(own_sums, 'met', 0, 0, axis_index_groups=[ROWS_ORDER])]
where the time goes in v6:
time: 49.9 us; the launch traced here: 49.6 us
  blocking collectives  34.5 us (69%)
  Pallas kernels  8.94 us (18%)
  starting transfers between devices  4.85 us (10%)
  waiting for transfers between devices  0.66 us (1%)
  between operations  0.65 us (1%)
    all_to_all x1, blocking collectives, local(): lax.all_to_all(copies, 'mach', 0, 0, axis_index_groups=plane_order)  19.1 us
    all_to_all x1, blocking collectives, local(): lax.all_to_all(partial, 'met', 0, 0, axis_index_groups=[SUMS_ORDER])  15.4 us
    all_to_all x1, starting transfers between devices, local(): sums = lax.all_to_all(own_sums, 'met', 0, 0, axis_index_groups=[ROWS_ORDER])  4.85 us
    pallas_call x1, Pallas kernels, local(): pl.pallas_call(solve_kernel, out_shape=(jax.ShapeDtypeStruct((steps, 4 *...  3.92 us
    pallas_call x1, Pallas kernels, local(): pl.pallas_call(residual_kernel, out_shape=jax.ShapeDtypeStruct(tensor.sha...  1.76 us
    pallas_call x1, Pallas kernels, local(): pl.pallas_call(begin_kernel, out_shape=(jax.ShapeDtypeStruct((plane, rows...  1.65 us
  transfers between devices with their start and end apart: 1, of which 1 were waited for; matrix products, arithmetic and copies ran while one was open for 0% of the time, Pallas kernels for 8%

profile of v6, /device:TPU:1, one launch (start us, length us, event | category | flops | bytes accessed | tf_op | source)
XLA Modules:
  0.0 49.6 jit_solution(17469477990316715286)
XLA Ops:
  0.6 1.6 %shard_map.50 = (f32[64,2,128]{2,1,0:T(2,128)S(1)}, f32[4,512,256]{2,1,0:T(8,128)S(1)}, f32[4,64]{1,0:T(4,128)S(1)}, f32[64,64]{1,0:T(8,128)S(1)}) custom-call(f32[4,64]{1,0:T(4,128)} %m_hbm.1, f32[4,512,256]{2,1,0:T(8,128)} %t_hbm.1, f32[4,64]{1,0:T(4,128)} %tf_hbm.1), custom_call_target="tpu_custom_call" | custom-call | tf_op jit(solution)/shard_map/pallas_call | solution.py:232
  2.3 19.1 %all_to_all.15 = f32[64,2,128]{2,1,0:T(2,128)S(1)} all-to-all(f32[64,2,128]{2,1,0:T(2,128)S(1)} %get-tuple-element.13), channel_id=1, replica_groups={{37,38,39,40,41,42,43,44,45,46,47,48,49,50,51,52,53,54,55,56,57,58,59,6..., dimensions={0} | all-to-all | bytes 131072 | tf_op jit(solution)/shard_map/all_to_all | solution.py:254
  21.4 0.9 %shard_map.51 = (f32[8,56,128]{2,1,0:T(8,128)S(1)}, f32[256,128]{1,0:T(8,128)S(1)}) custom-call(f32[4,512,256]{2,1,0:T(8,128)S(1)} %get-tuple-element.12.t_ref, f32[128,128]{1,0:T(8,128)S(1)} %bitcast.1, f32[4,64]{1,0:T(4,128)S(1)} %get-tuple-element.14.tf_ref), custom_call_target="tpu_custom_call" | custom-call | tf_op jit(solution)/shard_map/pallas_call | solution.py:258
  22.3 15.4 %all_to_all.16.r_ref = f32[8,56,128]{2,1,0:T(8,128)S(1)} all-to-all(f32[8,56,128]{2,1,0:T(8,128)S(1)} %get-tuple-element.15), channel_id=1, replica_groups={{384,128,448,192,320,0,64,256},{385,129,449,193,321,1,65,257},{386,130,..., dimensions={0} | all-to-all | bytes 458752 | tf_op jit(solution)/shard_map/all_to_all | solution.py:268
  37.7 0.7 %shard_map.52 = (f32[8,32,128]{2,1,0:T(8,128)}, f32[24,128]{1,0:T(8,128)S(1)}) custom-call(f32[8,56,128]{2,1,0:T(8,128)S(1)} %all_to_all.16.r_ref), custom_call_target="tpu_custom_call" | custom-call | tf_op jit(solution)/shard_map/pallas_call | solution.py:269
  38.4 4.8 %all-to-all-start.2 = ((f32[8,32,128]{2,1,0:T(8,128)}), f32[8,32,128]{2,1,0:T(8,128)S(1)}, u32[]{:S(2)}, u32[]{:S(2)}) async-start(f32[8,32,128]{2,1,0:T(8,128)} %get-tuple-element.17.own_ref), calls=%async_computation.2 | async-start | bytes 262144 | tf_op jit(solution)/shard_map/all_to_all | solution.py:279
  43.2 3.9 %shard_map.53 = (bf16[4,256,256]{2,1,0:T(8,128)(2,1)S(1)}, f32[64,64]{1,0:T(8,128)}) custom-call(f32[24,128]{1,0:T(8,128)S(1)} %get-tuple-element.16.gram_ref, f32[8,32,128]{2,1,0:T(8,128)} %get-tuple-element.17.own_ref, f32[256,128]{1,0:T(8,128)S(1)} %get-tuple-element.18.m_ref, f32[4,64]{1,0:T(4,128)S(1)} %get-tuple-element.14.tf_ref, ...), custom_call_target="tpu_custom_call" | custom-call | flops 1000000000 | bytes 10000000 | tf_op jit(solution)/shard_map/pallas_call | solution.py:280
  47.2 0.7 %all-to-all-done.2.s_ref = f32[8,32,128]{2,1,0:T(8,128)S(1)} async-done(((f32[8,32,128]{2,1,0:T(8,128)}), f32[8,32,128]{2,1,0:T(8,128)S(1)}, u32[]{:S(2)}, u32[]{:S(2)}) %all-to-all-start.2) | async-done | bytes 131104 | tf_op jit(solution)/shard_map/all_to_all | solution.py:279
  47.8 1.8 %shard_map.54 = f32[4,512,256]{2,1,0:T(8,128)} custom-call(f32[4,512,256]{2,1,0:T(8,128)S(1)} %get-tuple-element.12.t_ref, f32[8,32,128]{2,1,0:T(8,128)S(1)} %all-to-all-done.2.s_ref, bf16[4,256,256]{2,1,0:T(8,128)(2,1)S(1)} %get-tuple-element.21.w_ref), custom_call_target="tpu_custom_call" | custom-call | tf_op jit(solution)/shard_map/pallas_call | solution.py:291
Async XLA Ops:
  38.4 9.4 %all-to-all-start.2 = ((f32[8,32,128]{2,1,0:T(8,128)}), f32[8,32,128]{2,1,0:T(8,128)S(1)}, u32[]{:S(2)}, u32[]{:S(2)}) async-start(f32[8,32,128]{2,1,0:T(8,128)} %get-tuple-element.17.own_ref), calls=%async_computation.2 | async-start | bytes 262144 | tf_op jit(solution)/shard_map/all_to_all | solution.py:279
